TPU v7x, 32 devices: a whole 2x2x4 slice. The times are simulated.
32 devices in a mesh: dp: 4 (over z), seq: 8 (over y, x, core).
Axes of the slice: x: 2, y: 2, z: 4, core: 2. Of those that a mesh axis runs over, the one named last changes fastest.
Arguments:
- tokens: bfloat16 [4, 2048, 2048], P('dp', 'seq'), may hold values from -6 to 6
- cotangent: bfloat16 [4, 2048, 2048], P('dp', 'seq'), may hold values from -6 to 6
- kernel: bfloat16 [2048, 2048], P('seq'), may hold values from -6 to 6
- first_factor: bfloat16 [8, 256, 256], P('seq'), may hold values from -0.375 to 0.375
- second_factor: bfloat16 [256, 8, 8], P('seq'), may hold values from -2 to 2
Outputs:
- grad_kernel: bfloat16 [2048, 2048], P('seq')
- grad_first: float32 [8, 256, 256], P('seq')
- grad_second: float32 [256, 8, 8], P('seq')
All inputs are finite; a program needn't handle non-finite values.
Results may differ from a plain program's by a relative error of at most 0.0058.
Values may be sent and summed in bfloat16 or wider, within the bound.
A program may use at most 64 MiB of HBM per device.

v0:
```python
import math

import jax
import jax.numpy as jnp
from jax import lax
from jax.sharding import PartitionSpec as P


def shards(tokens, cotangent, kernel, first_factor, second_factor):
    local_rows = tokens.shape[1]
    channels = tokens.shape[2]
    column_blocks = second_factor.shape[0]
    mixed_in = jnp.einsum(
        "aqb,abc->aqc", first_factor, tokens, preferred_element_type=jnp.float32
    ).astype(jnp.bfloat16)
    mixed_up = jnp.einsum(
        "aqb,abc->aqc", first_factor, cotangent, preferred_element_type=jnp.float32
    ).astype(jnp.bfloat16)
    arrived_in = lax.all_to_all(mixed_in, "seq", split_axis=1, concat_axis=0, tiled=True)
    arrived_up = lax.all_to_all(mixed_up, "seq", split_axis=1, concat_axis=0, tiled=True)
    forward = jnp.einsum(
        "bpa,abc->bpc", second_factor, arrived_in, preferred_element_type=jnp.float32
    )
    backward = jnp.einsum(
        "bpa,abc->bpc", second_factor, arrived_up, preferred_element_type=jnp.float32
    )
    arrived_in, arrived_up, forward, backward = (arrived_in, arrived_up, forward, backward)
    kernel_local = kernel.reshape(column_blocks, -1, channels)
    kernel_grad = forward * backward
    weighted = (kernel_local * forward).astype(jnp.bfloat16)
    pulled = (kernel_local * backward).astype(jnp.bfloat16)
    second_grad = jnp.einsum(
        "bpc,abc->bpa", pulled, arrived_in, preferred_element_type=jnp.float32
    ) + jnp.einsum("bpc,abc->bpa", weighted, arrived_up, preferred_element_type=jnp.float32)
    spread = jnp.einsum(
        "bpa,bpc->abc", second_factor, weighted, preferred_element_type=jnp.float32
    ).astype(jnp.bfloat16)
    pulled_back = jnp.einsum(
        "bpa,bpc->abc", second_factor, pulled, preferred_element_type=jnp.float32
    ).astype(jnp.bfloat16)
    seq_share = 1.0 / math.sqrt(lax.axis_size("dp"))
    factor_share = 1.0 / math.sqrt(2.0 * channels * lax.axis_size("dp"))
    returned, returned_back = (
        lax.all_to_all(spread, "seq", split_axis=0, concat_axis=1, tiled=True),
        lax.all_to_all(pulled_back, "seq", split_axis=0, concat_axis=1, tiled=True),
    )
    first_grad = jnp.einsum(
        "aqc,abc->aqb", returned_back, tokens, preferred_element_type=jnp.float32
    ) + jnp.einsum("aqc,abc->aqb", returned, cotangent, preferred_element_type=jnp.float32)
    kernel_total, first_total, second_total = lax.psum((kernel_grad, first_grad, second_grad), "dp")
    kernel_out = (kernel_total * seq_share).astype(jnp.bfloat16)
    return (
        kernel_out.reshape(local_rows, channels),
        first_total * factor_share,
        second_total * factor_share,
    )


def solution(mesh):
    in_specs = (
        P("dp", "seq", None),
        P("dp", "seq", None),
        P("seq", None),
        P("seq", None, None),
        P("seq", None, None),
    )
    out_specs = (P("seq", None), P("seq", None, None), P("seq", None, None))
    return jax.shard_map(shards, mesh=mesh, in_specs=in_specs, out_specs=out_specs, check_vma=False)
```

profile of v0, /device:TPU:0, one launch (start us, length us, event | category | flops | bytes accessed | tf_op | source)
XLA Modules:
  0.0 214.2 jit_solution(9006451979799711186)
XLA Ops:
  7.2 0.0 copy-start
  7.2 1.8 fusion.1
  9.0 1.6 copy.64
  10.6 0.5 broadcast
  11.1 7.8 %reduce = bf16[256,2048]{1,0:T(8,128)(2,1)} reduce(bf16[256,1,2048]{2,1,0:T(2,128)(2,1)S(1)} %bitcast.63, bf16[]{:T(256)} %broadcast), dimensions={1}, to_apply=%bitcast.55.reduce_sub_computation | reduce | bytes 2097154
  18.9 2.7 %reshape.60 = bf16[8,2,32768]{2,1,0:T(2,128)(2,1)} reshape(bf16[256,2048]{1,0:T(8,128)(2,1)} %reduce) | data formatting | bytes 2097152
  21.6 5.2 %all-to-all-start.1 = ((bf16[8,2,32768]{2,1,0:T(2,128)(2,1)}), bf16[8,2,32768]{2,1,0:T(2,128)(2,1)}, u32[]{:S(2)}, u32[]{:S(2)}) async-start(bf16[8,2,32768]{2,1,0:T(2,128)(2,1)} %reshape.60), calls=%async_computation.1 | async-start | bytes 2097152 | tf_op jit(solution)/shard_map/all_to_all | solution.py:20
  26.8 0.4 fusion
  27.2 1.6 copy.65
  28.8 7.8 %reduce.1 = bf16[256,2048]{1,0:T(8,128)(2,1)} reduce(bf16[256,1,2048]{2,1,0:T(2,128)(2,1)S(1)} %bitcast.64, bf16[]{:T(256)} %broadcast), dimensions={1}, to_apply=%bitcast.56.reduce_sub_computation | reduce | bytes 2097154
  36.6 2.6 %reshape.58 = bf16[8,2,32768]{2,1,0:T(2,128)(2,1)} reshape(bf16[256,2048]{1,0:T(8,128)(2,1)} %reduce.1) | data formatting | bytes 2097152
  39.2 3.0 %all-to-all-done.1 = bf16[8,2,32768]{2,1,0:T(2,128)(2,1)} async-done(((bf16[8,2,32768]{2,1,0:T(2,128)(2,1)}), bf16[8,2,32768]{2,1,0:T(2,128)(2,1)}, u32[]{:S(2)}, u32[]{:S(2)}) %all-to-all-start.1) | async-done | bytes 1048608 | tf_op jit(solution)/shard_map/all_to_all | solution.py:20
  42.3 4.3 %all-to-all-start = ((bf16[8,2,32768]{2,1,0:T(2,128)(2,1)}), bf16[8,2,32768]{2,1,0:T(2,128)(2,1)}, u32[]{:S(2)}, u32[]{:S(2)}) async-start(bf16[8,2,32768]{2,1,0:T(2,128)(2,1)} %reshape.58), calls=%async_computation | async-start | bytes 2097152 | tf_op jit(solution)/shard_map/all_to_all | solution.py:19
  46.5 0.0 copy-done.11
  46.5 0.1 copy.43
  46.7 4.3 %reshape.61 = bf16[256,1,2048]{2,1,0:T(2,128)(2,1)S(1)} reshape(bf16[8,2,32768]{2,1,0:T(2,128)(2,1)} %all-to-all-done.1) | data formatting | bytes 2097152
  51.0 0.6 copy.51
  51.6 0.0 copy-start.3
  51.6 1.0 copy-done.6
  52.6 0.8 convolution_bitcast_fusion
  53.4 0.0 copy-done.3
  53.4 0.5 fusion.2
  53.9 1.5 copy.44
  55.4 6.5 %all-to-all-done = bf16[8,2,32768]{2,1,0:T(2,128)(2,1)} async-done(((bf16[8,2,32768]{2,1,0:T(2,128)(2,1)}), bf16[8,2,32768]{2,1,0:T(2,128)(2,1)}, u32[]{:S(2)}, u32[]{:S(2)}) %all-to-all-start) | async-done | bytes 1048608 | tf_op jit(solution)/shard_map/all_to_all | solution.py:19
  61.9 4.5 %all-to-all-start.2 = ((bf16[8,32,2048]{2,1,0:T(8,128)(2,1)}), bf16[8,32,2048]{2,1,0:T(8,128)(2,1)}, u32[]{:S(2)}, u32[]{:S(2)}) async-start(bf16[8,32,2048]{2,1,0:T(8,128)(2,1)} %copy.44), calls=%async_computation.2 | async-start | bytes 2097152 | tf_op jit(solution)/shard_map/all_to_all | solution.py:45
  66.4 5.8 %reshape.59 = bf16[256,1,2048]{2,1,0:T(2,128)(2,1)} reshape(bf16[8,2,32768]{2,1,0:T(2,128)(2,1)} %all-to-all-done) | data formatting | bytes 2097152
  72.2 2.2 %copy.50 = bf16[1,256,2048]{2,1,0:T(8,128)(2,1)S(1)} copy(bf16[1,256,2048]{2,0,1:T(2,128)(2,1)} %bitcast.62) | data formatting | bytes 2097152
  74.4 0.0 copy-start.4
  74.4 2.2 %fusion.24 = (f32[32,8,2048]{2,1,0:T(8,128)}, f32[32,8,2048]{2,1,0:T(8,128)S(1)}) fusion(f32[32,8,2048]{2,1,0:T(8,128)S(1)} %convolution_bitcast_fusion, bf16[32,8,8]{1,2,0:T(8,128)(2,1)S(1)} %copy.43, bf16[8,32,2048]{2,1,0:T(8,128)(2,1)S(1)} %bitcast.59), kind=kOutput, calls=%fused_computation.33 | convolution fusion | flops 8912896 | bytes 7344128 | tf_op jit(solution)/shard_map/bpa,abc->bpc/dot_general | solution.py:21
  76.7 0.4 fusion.3
  77.1 0.9 copy-done.1
  78.0 1.6 copy.46
  79.6 2.0 all-to-all-done.2
  81.6 4.3 %all-to-all-start.3 = ((bf16[8,32,2048]{2,1,0:T(8,128)(2,1)}), bf16[8,32,2048]{2,1,0:T(8,128)(2,1)}, u32[]{:S(2)}, u32[]{:S(2)}) async-start(bf16[8,32,2048]{2,1,0:T(8,128)(2,1)} %copy.46), calls=%async_computation.3 | async-start | bytes 2097152 | tf_op jit(solution)/shard_map/all_to_all | solution.py:44
  85.9 0.0 all-reduce.3.cloned.1.call-start
  85.9 1.7 fusion.10
  87.6 13.7 %all-to-all-done.3 = bf16[8,32,2048]{2,1,0:T(8,128)(2,1)} async-done(((bf16[8,32,2048]{2,1,0:T(8,128)(2,1)}), bf16[8,32,2048]{2,1,0:T(8,128)(2,1)}, u32[]{:S(2)}, u32[]{:S(2)}) %all-to-all-start.3) | async-done | bytes 1048608 | tf_op jit(solution)/shard_map/all_to_all | solution.py:44
  101.3 2.7 %fusion.6 = f32[1,256,256]{2,1,0:T(8,128)} fusion(f32[256,256]{1,0:T(8,128)S(1)} %fusion.10, bf16[256,2048]{1,0:T(8,128)(2,1)} %bitcast.13, bf16[1,256,2048]{2,1,0:T(8,128)(2,1)} %param.6), kind=kOutput, calls=%fused_computation.16 | convolution fusion | flops 268500992 | bytes 2621440 | tf_op jit(solution)/shard_map/aqc,abc->aqb/dot_general | solution.py:49
  104.0 0.0 all-reduce.3.cloned.1.call-update
  104.1 0.0 copy-start.5
  104.1 2.6 %fusion.15 = f32[32,8,8]{2,1,0:T(8,128)S(1)} fusion(bf16[8,32,2048]{2,1,0:T(8,128)(2,1)} %bitcast.60, f32[32,8,2048]{2,1,0:T(8,128)S(1)} %convolution_bitcast_fusion, bf16[256,2048]{1,0:T(8,128)(2,1)} %param.7), kind=kOutput, calls=%fused_computation.26 | convolution fusion | flops 9961472 | bytes 4202496 | tf_op jit(solution)/shard_map/bpc,abc->bpa/dot_general | solution.py:32
  106.7 0.2 copy-done.7
  106.9 0.8 convolution_add_fusion.1
  107.6 25.6 %psum.23 = f32[32,8,8]{2,1,0:T(8,128)S(1)} all-reduce(f32[32,8,8]{2,1,0:T(8,128)S(1)} %convolution_add_fusion.1), channel_id=1, replica_groups=mesh['dp'=4,'seq'=8] {'dp'}, use_global_device_ids=true, to_apply=%region_2.0 | all-reduce | flops 2048 | bytes 16384 | tf_op jit(solution)/shard_map/psum | solution.py:50
  133.2 0.7 copy.49
  133.9 69.9 %all-reduce.3.cloned.1.call-done = (f32[32,8,2048]{2,1,0:T(8,128)}, f32[1,256,256]{2,1,0:T(8,128)}) async-done(((f32[32,8,2048]{2,1,0:T(8,128)}, f32[1,256,256]{2,1,0:T(8,128)}), (f32[32,8,2048]{2,1,0:T(8,128)}, f32[1,256,256]{2,1,0:T(8,128)})) %all-reduce.3.cloned.1.call-update) | async-done | bytes 2359312 | tf_op jit(solution)/shard_map/psum | solution.py:50
  203.8 2.8 %fusion.7 = bf16[256,2048]{1,0:T(8,128)(2,1)} fusion(f32[32,8,2048]{2,1,0:T(8,128)} %get-tuple-element.15), kind=kLoop, calls=%fused_computation.18 | loop fusion | flops 1048576 | bytes 3145728 | tf_op jit(solution)/shard_map/reshape | solution.py:53
  206.6 0.7 broadcast_multiply_fusion
  (16 shorter events, 0.0 us)
Async XLA Ops:
  7.2 19.6 %copy-start = (bf16[1,256,2048]{2,1,0:T(8,128)(2,1)S(1)}, bf16[1,256,2048]{2,1,0:T(8,128)(2,1)}, u32[]{:S(2)}) copy-start(bf16[1,256,2048]{2,1,0:T(8,128)(2,1)} %param.5) | copy-start | bytes 3145732
  18.9 7.8 %copy-start.9 = (bf16[1,256,256]{2,1,0:T(8,128)(2,1)S(1)}, bf16[1,256,256]{2,1,0:T(8,128)(2,1)}, u32[]{:S(2)}) copy-start(bf16[1,256,256]{2,1,0:T(8,128)(2,1)} %param.8) | copy-start | bytes 393220
  21.6 20.7 %all-to-all-start.1 = ((bf16[8,2,32768]{2,1,0:T(2,128)(2,1)}), bf16[8,2,32768]{2,1,0:T(2,128)(2,1)}, u32[]{:S(2)}, u32[]{:S(2)}) async-start(bf16[8,2,32768]{2,1,0:T(2,128)(2,1)} %reshape.60), calls=%async_computation.1 | async-start | bytes 2097152 | tf_op jit(solution)/shard_map/all_to_all | solution.py:20
  36.6 9.9 %copy-start.11 = (bf16[32,8,8]{0,2,1:T(8,128)(2,1)S(1)}, bf16[32,8,8]{0,2,1:T(8,128)(2,1)}, u32[]{:S(2)}) copy-start(bf16[32,8,8]{0,2,1:T(8,128)(2,1)} %param.9) | copy-start | bytes 12292
  42.3 19.7 %all-to-all-start = ((bf16[8,2,32768]{2,1,0:T(2,128)(2,1)}), bf16[8,2,32768]{2,1,0:T(2,128)(2,1)}, u32[]{:S(2)}, u32[]{:S(2)}) async-start(bf16[8,2,32768]{2,1,0:T(2,128)(2,1)} %reshape.58), calls=%async_computation | async-start | bytes 2097152 | tf_op jit(solution)/shard_map/all_to_all | solution.py:19
  51.6 1.0 copy-start.6
  51.6 1.8 copy-start.3
  61.9 19.7 %all-to-all-start.2 = ((bf16[8,32,2048]{2,1,0:T(8,128)(2,1)}), bf16[8,32,2048]{2,1,0:T(8,128)(2,1)}, u32[]{:S(2)}, u32[]{:S(2)}) async-start(bf16[8,32,2048]{2,1,0:T(8,128)(2,1)} %copy.44), calls=%async_computation.2 | async-start | bytes 2097152 | tf_op jit(solution)/shard_map/all_to_all | solution.py:45
  74.4 2.2 %copy-start.8 = (bf16[1,256,2048]{2,1,0:T(8,128)(2,1)}, bf16[1,256,2048]{2,1,0:T(8,128)(2,1)S(1)}, u32[]{:S(2)}) copy-start(bf16[1,256,2048]{2,1,0:T(8,128)(2,1)S(1)} %copy.50) | copy-start | bytes 3145732
  74.4 2.2 %copy-start.4 = (bf16[256,2048]{1,0:T(8,128)(2,1)S(1)}, bf16[256,2048]{1,0:T(8,128)(2,1)}, u32[]{:S(2)}) copy-start(bf16[256,2048]{1,0:T(8,128)(2,1)} %param.7) | copy-start | bytes 3145732
  76.7 1.3 copy-start.1
  81.6 19.7 %all-to-all-start.3 = ((bf16[8,32,2048]{2,1,0:T(8,128)(2,1)}), bf16[8,32,2048]{2,1,0:T(8,128)(2,1)}, u32[]{:S(2)}, u32[]{:S(2)}) async-start(bf16[8,32,2048]{2,1,0:T(8,128)(2,1)} %copy.46), calls=%async_computation.3 | async-start | bytes 2097152 | tf_op jit(solution)/shard_map/all_to_all | solution.py:44
  85.9 117.9 %all-reduce.3.cloned.1.call-start = ((), (), s32[]{:S(2)}) async-start(), calls=%async_computation.4 | async-start | bytes 4718592 | tf_op jit(solution)/shard_map/psum | solution.py:50
  104.1 2.6 %copy-start.2 = (f32[32,8,2048]{2,1,0:T(8,128)S(1)}, f32[32,8,2048]{2,1,0:T(8,128)}, u32[]{:S(2)}) copy-start(f32[32,8,2048]{2,1,0:T(8,128)} %copy-done.1) | copy-start | bytes 6291460
  104.1 2.6 %copy-start.5 = (bf16[256,2048]{1,0:T(8,128)(2,1)S(1)}, bf16[256,2048]{1,0:T(8,128)(2,1)}, u32[]{:S(2)}) copy-start(bf16[256,2048]{1,0:T(8,128)(2,1)} %param.7) | copy-start | bytes 3145732
  104.1 2.8 %copy-start.7 = (bf16[1,256,2048]{2,1,0:T(8,128)(2,1)S(1)}, bf16[1,256,2048]{2,1,0:T(8,128)(2,1)}, u32[]{:S(2)}) copy-start(bf16[1,256,2048]{2,1,0:T(8,128)(2,1)} %copy-done.6) | copy-start | bytes 3145732
  203.8 2.8 %copy-start.10 = (f32[1,256,256]{2,1,0:T(8,128)S(1)}, f32[1,256,256]{2,1,0:T(8,128)}, u32[]{:S(2)}) copy-start(f32[1,256,256]{2,1,0:T(8,128)} %get-tuple-element.16) | copy-start | bytes 786436
Sparse Core Ops, SparseCore 0:
  104.2 99.6 all-reduce.2
where the time goes:
time: 215 us; the launch traced here: 214 us
  waiting for transfers between devices  95.1 us (44%)
  local copies, waits for them, and re-layouts  28.1 us (13%)
  blocking collectives  25.6 us (12%)
  other arithmetic  19 us (9%)
  starting transfers between devices  18.2 us (8%)
  between operations  14.2 us (7%)
  matrix products  14 us (7%)
    psum x1, waiting for transfers between devices, shards(): lax.psum((kernel_grad, first_grad, second_grad), 'dp')  69.9 us
    psum x1, blocking collectives, shards(): lax.psum((kernel_grad, first_grad, second_grad), 'dp')  25.6 us
    unnamed x33, local copies, waits for them, and re-layouts  21.7 us
    unnamed x2, other arithmetic  15.5 us
    all_to_all x1, waiting for transfers between devices, shards(): lax.all_to_all(spread, 'seq', split_axis=0, concat_axis=1, tiled=True)  13.7 us
    all_to_all x1, waiting for transfers between devices, shards(): lax.all_to_all(mixed_in, 'seq', split_axis=1, concat_axis=0, tiled=True)  6.5 us
    all_to_all x1, starting transfers between devices, shards(): lax.all_to_all(mixed_up, 'seq', split_axis=1, concat_axis=0, tiled=True)  5.17 us
    all_to_all x1, starting transfers between devices, shards(): lax.all_to_all(pulled_back, 'seq', split_axis=0, concat_axis=1, tiled=True)  4.47 us
  transfers between devices with their start and end apart: 5, of which 5 were waited for; matrix products, arithmetic and copies ran while one was open for 18% of the time, Pallas kernels for 0%

commit v1 on v0

--- a/solution.py
+++ b/solution.py
@@ -1,12 +1,394 @@
+import functools
 import math
 
 import jax
 import jax.numpy as jnp
 from jax import lax
+from jax.experimental import pallas as pl
+from jax.experimental.pallas import tpu as pltpu
 from jax.sharding import PartitionSpec as P
 
-
-def shards(tokens, cotangent, kernel, first_factor, second_factor):
+MESH = pl.DeviceIdType.MESH
+BF16 = jnp.bfloat16
+F32 = jnp.float32
+HALVES = 2
+CHUNKS = 4
+
+
+def dot(left, right):
+    return jnp.dot(left, right, preferred_element_type=F32)
+
+
+def dot_rows(left, right):
+    return lax.dot_general(left, right, (((1,), (1,)), ((), ())), preferred_element_type=F32)
+
+
+def mixer_kernel(
+    n,
+    groups,
+    chunks,
+    seq_share,
+    factor_share,
+    tokens_ref,
+    cotangent_ref,
+    kernel_ref,
+    first_ref,
+    second_ref,
+    kernel_out,
+    first_out,
+    second_out,
+    first_v,
+    tokens_v,
+    cotangent_v,
+    kernel_v,
+    factor_v,
+    factor_t_v,
+    mixed,
+    arrived,
+    spread,
+    returned,
+    own_terms,
+    outer_terms,
+    pair_terms,
+    other_terms,
+    final_terms,
+    second_acc,
+    second_terms,
+    first_acc,
+    first_terms,
+    load_sem,
+    first_load_sem,
+    store_sem,
+    out_send,
+    out_recv,
+    back_send,
+    back_recv,
+    outer_send,
+    outer_recv,
+    pair_send,
+    pair_recv,
+    final_send,
+    final_recv,
+    second_send,
+    second_recv,
+    first_send,
+    first_recv,
+):
+    me = lax.axis_index("seq")
+    z = lax.axis_index("dp")
+    inner = jnp.logical_and(z >= 1, z <= 2)
+    outer = jnp.logical_not(inner)
+    rows = first_v.shape[0]
+    width = tokens_v.shape[2]
+    block = rows // n
+    part = block // HALVES
+
+    first_load = pltpu.make_async_copy(first_ref.at[0], first_v, first_load_sem)
+    first_load.start()
+    loads = []
+    for k in range(chunks):
+        columns = pl.ds(k * width, width)
+        trio = [
+            pltpu.make_async_copy(tokens_ref.at[0, :, columns], tokens_v.at[k], load_sem.at[k, 0]),
+            pltpu.make_async_copy(cotangent_ref.at[0, :, columns], cotangent_v.at[k], load_sem.at[k, 1]),
+            pltpu.make_async_copy(kernel_ref.at[:, columns], kernel_v.at[k], load_sem.at[k, 2]),
+        ]
+        trio[0].start()
+        trio[1].start()
+        loads.append(trio)
+    for trio in loads:
+        trio[2].start()
+
+    barrier = pltpu.get_barrier_semaphore()
+    for d in range(1, n):
+        pl.semaphore_signal(barrier, inc=1, device_id={"seq": lax.rem(me + d, n)}, device_id_type=MESH)
+    for d in range(1, groups):
+        pl.semaphore_signal(barrier, inc=1, device_id={"dp": lax.rem(z + d, groups)}, device_id_type=MESH)
+
+    shape = (n, block, rows)
+    row_block = lax.broadcasted_iota(jnp.int32, shape, 1) * n
+    column = lax.broadcasted_iota(jnp.int32, shape, 2)
+    same_block = jnp.logical_and(column >= row_block, column < row_block + n)
+    spread_factor = jnp.broadcast_to(second_ref[...][:, None, :], shape)
+    transposed = jnp.where(same_block, spread_factor, 0.0).reshape(rows, rows)
+    factor_t_v[...] = transposed.astype(BF16)
+    factor_v[...] = transposed.T.astype(BF16)
+    second_acc[...] = jnp.zeros_like(second_acc)
+
+    def out_copy(k, source, target):
+        return pltpu.make_async_remote_copy(
+            src_ref=mixed.at[k, target],
+            dst_ref=arrived.at[k, source],
+            send_sem=out_send.at[k, target],
+            recv_sem=out_recv.at[k, source],
+            device_id={"seq": target},
+            device_id_type=MESH,
+        )
+
+    def back_copy(h, k, source, target):
+        return pltpu.make_async_remote_copy(
+            src_ref=spread.at[h, k, target],
+            dst_ref=returned.at[h, k, source],
+            send_sem=back_send.at[h, k, target],
+            recv_sem=back_recv.at[h, k, source],
+            device_id={"seq": target},
+            device_id_type=MESH,
+        )
+
+    def line_copy(src, dst, send, recv, target):
+        return pltpu.make_async_remote_copy(
+            src_ref=src,
+            dst_ref=dst,
+            send_sem=send,
+            recv_sem=recv,
+            device_id={"dp": target},
+            device_id_type=MESH,
+        )
+
+    inner_partner = 1 + z // 3
+    outer_partner = (z - 1) * 3
+    other_inner = 3 - z
+
+    def outer_copy(k):
+        return line_copy(pair_terms.at[k], outer_terms.at[k], outer_send.at[k], outer_recv.at[k], inner_partner)
+
+    def pair_copy(k):
+        return line_copy(pair_terms.at[k], other_terms.at[k], pair_send.at[k], pair_recv.at[k], other_inner)
+
+    def final_copy(k):
+        return line_copy(final_terms.at[k], final_terms.at[k], final_send.at[k], final_recv.at[k], outer_partner)
+
+    def second_copy(source, target):
+        return line_copy(
+            second_terms.at[source], second_terms.at[source], second_send.at[target], second_recv.at[source], target
+        )
+
+    def first_copy(h, source, target):
+        return line_copy(
+            first_terms.at[h, source], first_terms.at[h, source], first_send.at[h, target], first_recv.at[h, source], target
+        )
+
+    def peers(action):
+        def step(d, carry):
+            action(lax.rem(me + d, n))
+            return carry
+
+        lax.fori_loop(1, n, step, 0)
+
+    def line_peers(action):
+        for d in range(1, groups):
+            action(lax.rem(z + d, groups))
+
+    first_load.wait()
+    for k in range(chunks):
+        loads[k][0].wait()
+        loads[k][1].wait()
+        mixed[k, :, 0] = dot(first_v[...], tokens_v[k]).astype(BF16).reshape(n, block, width)
+        mixed[k, :, 1] = dot(first_v[...], cotangent_v[k]).astype(BF16).reshape(n, block, width)
+        if k == 0:
+            pl.semaphore_wait(barrier, n + groups - 2)
+        peers(lambda target, k=k: out_copy(k, me, target).start())
+        arrived[k, me] = mixed[k, me]
+    for trio in loads:
+        trio[2].wait()
+
+    def make_pair(k):
+        outer_copy(k).wait_recv()
+        pair_terms[k] = (own_terms[k] + outer_terms[k].astype(F32)).astype(BF16)
+        pair_copy(k).start()
+
+    def make_final(k):
+        pair_copy(k).wait_recv()
+        total = pair_terms[k].astype(F32) + other_terms[k].astype(F32)
+        final_terms[k] = (total * seq_share).astype(BF16)
+        final_copy(k).start()
+
+    def transform(k, carry):
+        peers(lambda source: out_copy(k, source, me).wait_recv())
+        mixed_in = arrived[k, :, 0].reshape(rows, width)
+        mixed_up = arrived[k, :, 1].reshape(rows, width)
+        forward = dot(factor_v[...], mixed_in)
+        backward = dot(factor_v[...], mixed_up)
+        terms = forward * backward
+        gains = kernel_v[k].astype(F32)
+        weighted = (gains * forward).astype(BF16)
+        pulled = (gains * backward).astype(BF16)
+        back = dot(factor_t_v[...], pulled).astype(BF16).reshape(n, HALVES, part, width)
+        ahead = dot(factor_t_v[...], weighted).astype(BF16).reshape(n, HALVES, part, width)
+        for h in range(HALVES):
+            spread[h, k, :, 0] = back[:, h]
+            spread[h, k, :, 1] = ahead[:, h]
+        peers(lambda target: back_copy(0, k, me, target).start())
+
+        @pl.when(outer)
+        def _():
+            pair_terms[k] = terms.astype(BF16)
+            outer_copy(k).start()
+
+        @pl.when(inner)
+        def _():
+            own_terms[k] = terms
+
+        for h in range(HALVES):
+            returned[h, k, me] = spread[h, k, me]
+        second_acc[...] += dot_rows(mixed_in, pulled) + dot_rows(mixed_up, weighted)
+
+        @pl.when(jnp.logical_and(inner, k >= 1))
+        def _():
+            make_pair(k - 1)
+
+        @pl.when(jnp.logical_and(inner, k >= 2))
+        def _():
+            make_final(k - 2)
+
+        return carry
+
+    lax.fori_loop(0, chunks, transform, 0)
+    for h in range(1, HALVES):
+        for k in range(chunks):
+            peers(lambda target, h=h, k=k: back_copy(h, k, me, target).start())
+
+    second_terms[z] = jnp.sum(
+        jnp.where(same_block, second_acc[...].reshape(shape), 0.0), axis=1
+    )
+    line_peers(lambda target: second_copy(z, target).start())
+
+    @pl.when(inner)
+    def _():
+        make_pair(chunks - 1)
+        if chunks >= 2:
+            make_final(chunks - 2)
+
+    for h in range(HALVES):
+        first_acc[...] = jnp.zeros_like(first_acc)
+
+        def gather(k, carry, h=h):
+            peers(lambda source: back_copy(h, k, source, me).wait_recv())
+            back = returned[h, k, :, 0].reshape(n * part, width)
+            ahead = returned[h, k, :, 1].reshape(n * part, width)
+            first_acc[...] += dot_rows(back, tokens_v[k]) + dot_rows(ahead, cotangent_v[k])
+            return carry
+
+        lax.fori_loop(0, chunks, gather, 0)
+        first_terms[h, z] = first_acc[...].astype(BF16)
+        line_peers(lambda target, h=h: first_copy(h, z, target).start())
+        if h == 0:
+
+            @pl.when(inner)
+            def _():
+                make_final(chunks - 1)
+
+    stores = []
+    for k in range(chunks):
+
+        @pl.when(outer)
+        def _():
+            final_copy(k).wait_recv()
+
+        stores.append(
+            pltpu.make_async_copy(final_terms.at[k], kernel_out.at[:, pl.ds(k * width, width)], store_sem.at[k])
+        )
+        stores[-1].start()
+
+    line_peers(lambda source: second_copy(source, z).wait_recv())
+    second_out[...] = jnp.sum(second_terms[...], axis=0) * factor_share
+    for h in range(HALVES):
+        line_peers(lambda source, h=h: first_copy(h, source, z).wait_recv())
+        total = jnp.sum(first_terms[h].astype(F32), axis=0) * factor_share
+        first_out[:, h] = total.reshape(n, part, rows)
+
+    for store in stores:
+        store.wait()
+    for k in range(chunks):
+        peers(lambda target, k=k: out_copy(k, me, target).wait_send())
+        for h in range(HALVES):
+            peers(lambda target, h=h, k=k: back_copy(h, k, me, target).wait_send())
+
+        @pl.when(outer)
+        def _():
+            outer_copy(k).wait_send()
+
+        @pl.when(inner)
+        def _():
+            pair_copy(k).wait_send()
+            final_copy(k).wait_send()
+
+    line_peers(lambda target: second_copy(z, target).wait_send())
+    for h in range(HALVES):
+        line_peers(lambda target, h=h: first_copy(h, z, target).wait_send())
+
+
+def fused(n, groups, tokens, cotangent, kernel, first_factor, second_factor):
+    rows, channels = tokens.shape[1:]
+    chunks = CHUNKS
+    width = channels // chunks
+    block = rows // n
+    part = block // HALVES
+    seq_share = 1.0 / math.sqrt(groups)
+    factor_share = 1.0 / math.sqrt(2.0 * channels * groups)
+    second = jnp.transpose(second_factor, (2, 0, 1)).reshape(n, rows).astype(F32)
+    any_spec = pl.BlockSpec(memory_space=pl.ANY)
+    vmem_spec = pl.BlockSpec(memory_space=pltpu.VMEM)
+    dma = pltpu.SemaphoreType.DMA
+    kernel_grad, first_grad, second_grad = pl.pallas_call(
+        functools.partial(mixer_kernel, n, groups, chunks, seq_share, factor_share),
+        out_shape=(
+            jax.ShapeDtypeStruct((rows, channels), BF16),
+            jax.ShapeDtypeStruct((n, HALVES, part, rows), F32),
+            jax.ShapeDtypeStruct((n, rows), F32),
+        ),
+        in_specs=[any_spec] * 4 + [vmem_spec],
+        out_specs=(any_spec, vmem_spec, vmem_spec),
+        scratch_shapes=[
+            pltpu.VMEM((rows, rows), BF16),
+            pltpu.VMEM((chunks, rows, width), BF16),
+            pltpu.VMEM((chunks, rows, width), BF16),
+            pltpu.VMEM((chunks, rows, width), BF16),
+            pltpu.VMEM((rows, rows), BF16),
+            pltpu.VMEM((rows, rows), BF16),
+            pltpu.VMEM((chunks, n, 2, block, width), BF16),
+            pltpu.VMEM((chunks, n, 2, block, width), BF16),
+            pltpu.VMEM((HALVES, chunks, n, 2, part, width), BF16),
+            pltpu.VMEM((HALVES, chunks, n, 2, part, width), BF16),
+            pltpu.VMEM((chunks, rows, width), F32),
+            pltpu.VMEM((chunks, rows, width), BF16),
+            pltpu.VMEM((chunks, rows, width), BF16),
+            pltpu.VMEM((chunks, rows, width), BF16),
+            pltpu.VMEM((chunks, rows, width), BF16),
+            pltpu.VMEM((rows, rows), F32),
+            pltpu.VMEM((groups, n, rows), F32),
+            pltpu.VMEM((n * part, rows), F32),
+            pltpu.VMEM((HALVES, groups, n * part, rows), BF16),
+            dma((chunks, 3)),
+            dma,
+            dma((chunks,)),
+            dma((chunks, n)),
+            dma((chunks, n)),
+            dma((HALVES, chunks, n)),
+            dma((HALVES, chunks, n)),
+            dma((chunks,)),
+            dma((chunks,)),
+            dma((chunks,)),
+            dma((chunks,)),
+            dma((chunks,)),
+            dma((chunks,)),
+            dma((groups,)),
+            dma((groups,)),
+            dma((HALVES, groups)),
+            dma((HALVES, groups)),
+        ],
+        compiler_params=pltpu.CompilerParams(
+            collective_id=0, has_side_effects=True, vmem_limit_bytes=48 * 1024 * 1024
+        ),
+        cost_estimate=pl.CostEstimate(
+            flops=16 * rows * rows * channels, bytes_accessed=8 * rows * channels, transcendentals=0
+        ),
+    )(tokens, cotangent, kernel, first_factor, second)
+    second_grad = second_grad.reshape(n, block, n).transpose(1, 2, 0)
+    return kernel_grad, first_grad.reshape(1, rows, rows), second_grad
+
+
+def separate(tokens, cotangent, kernel, first_factor, second_factor):
     local_rows = tokens.shape[1]
     channels = tokens.shape[2]
     column_blocks = second_factor.shape[0]
@@ -56,6 +438,22 @@
     )
 
 
+def shards(tokens, cotangent, kernel, first_factor, second_factor):
+    n = lax.axis_size("seq")
+    groups = lax.axis_size("dp")
+    rows, channels = tokens.shape[1:]
+    fits = (
+        groups == 4
+        and first_factor.shape[0] == 1
+        and second_factor.shape[1] == n
+        and second_factor.shape[0] % (16 * HALVES) == 0
+        and channels % (128 * CHUNKS) == 0
+        and rows == n * second_factor.shape[0]
+    )
+    arguments = (tokens, cotangent, kernel, first_factor, second_factor)
+    return fused(n, groups, *arguments) if fits else separate(*arguments)
+
+
 def solution(mesh):
     in_specs = (
         P("dp", "seq", None),

time: 215 us -> 74.2 us (0.35)
  waiting for transfers between devices: 95.1 us -> 0 us
  Pallas kernels: 0 us -> 65.5 us
  blocking collectives: 25.6 us -> 0 us
  local copies, waits for them, and re-layouts: 28.1 us -> 7.04 us
  other arithmetic: 19 us -> 0.72 us
  starting transfers between devices: 18.2 us -> 0 us
  matrix products: 14 us -> 0 us
  between operations: 14.2 us -> 0.66 us
    psum x1 -> x0, waiting for transfers between devices: 69.9 us -> none  [shards(): lax.psum((kernel_grad, first_grad, second_grad), 'dp')]
    pallas_call x0 -> x1, Pallas kernels: none -> 65.5 us  [fused(): pl.pallas_call(functools.partial(mixer_kernel, n, groups, chunks, seq_sha...]
    psum x1 -> x0, blocking collectives: 25.6 us -> none  [shards(): lax.psum((kernel_grad, first_grad, second_grad), 'dp')]
    all_to_all x4 -> x0, waiting for transfers between devices: 25.2 us -> none  [the longest x1 13.7 us: shards(): lax.all_to_all(spread, 'seq', split_axis=0, concat_axis=1, tiled=True)]
    all_to_all x4 -> x0, starting transfers between devices: 18.2 us -> none  [the longest x1 5.17 us: shards(): lax.all_to_all(mixed_up, 'seq', split_axis=1, concat_axis=0, tiled=True)]
    unnamed x2 -> x0, other arithmetic: 15.5 us -> none
    unnamed x33 -> x11, local copies, waits for them, and re-layouts: 21.7 us -> 6.73 us
    dot_general x10 -> x0, matrix products: 14 us -> none  [the longest x1 2.72 us: shards(): jnp.einsum('aqc,abc->aqb', returned, cotangent, preferred_element_type=jn...]
  transfers between devices with their start and end apart: 5 -> 0, of which waited for: 5 -> 0; matrix products, arithmetic and copies ran while one was open for 18% -> 0% of each run, Pallas kernels for 0% -> 0%
where the time goes in v1:
time: 74.2 us; the launch traced here: 73.9 us
  Pallas kernels  65.5 us (88%)
  local copies, waits for them, and re-layouts  7.04 us (9%)
    pallas_call x1, Pallas kernels, fused(): pl.pallas_call(functools.partial(mixer_kernel, n, groups, chunks, seq_sha...  65.5 us
    unnamed x11, local copies, waits for them, and re-layouts  6.73 us

profile of v1, /device:TPU:0, one launch (start us, length us, event | category | flops | bytes accessed | tf_op | source)
XLA Modules:
  0.0 73.9 jit_solution(4986320628305789479)
XLA Ops:
  0.6 0.7 convert_bitcast_fusion
  1.4 0.0 copy-start.3
  1.4 0.1 copy.10
  1.5 0.1 reshape.17.second_ref
  1.6 0.7 copy-done.3
  2.3 0.0 copy-start
  2.3 1.2 %copy-done = bf16[1,256,2048]{2,1,0:T(8,128)(2,1)S(1)} copy-done((bf16[1,256,2048]{2,1,0:T(8,128)(2,1)S(1)}, bf16[1,256,2048]{2,1,0:T(8,128)(2,1)}, u32[]{:S(2)}) %copy-start) | copy-done | bytes 1048600
  3.5 0.0 copy-start.1
  3.5 1.2 %copy-done.1 = bf16[1,256,2048]{2,1,0:T(8,128)(2,1)S(1)} copy-done((bf16[1,256,2048]{2,1,0:T(8,128)(2,1)S(1)}, bf16[1,256,2048]{2,1,0:T(8,128)(2,1)}, u32[]{:S(2)}) %copy-start.1) | copy-done | bytes 1048600
  4.7 0.0 copy-start.2
  4.7 1.2 %copy-done.2 = bf16[256,2048]{1,0:T(8,128)(2,1)S(1)} copy-done((bf16[256,2048]{1,0:T(8,128)(2,1)S(1)}, bf16[256,2048]{1,0:T(8,128)(2,1)}, u32[]{:S(2)}) %copy-start.2) | copy-done | bytes 1048600
  5.9 65.5 %shard_map.76 = (bf16[256,2048]{1,0:T(8,128)(2,1)S(1)}, f32[8,2,16,256]{3,2,1,0:T(8,128)S(1)}, f32[8,256]{1,0:T(8,128)S(1)}) custom-call(bf16[1,256,2048]{2,1,0:T(8,128)(2,1)S(1)} %copy-done, bf16[1,256,2048]{2,1,0:T(8,128)(2,1)S(1)} %copy-done.1, bf16[256,2048]{1,0:T(8,128)(2,1)S(1)} %copy-done.2, bf16[1,256,256]{2,1,0:T(8,128)(2,1)S(1)} %copy-done.3, ...), custom_call_target="tpu_custom_call" | custom-call | flops 2147483648 | bytes 4194304 | tf_op jit(solution)/shard_map/pallas_call | solution.py:333
  71.4 0.1 reshape.16
  71.5 0.7 copy.11
  72.2 1.0 %copy.14 = bf16[256,2048]{1,0:T(8,128)(2,1)} copy(bf16[256,2048]{1,0:T(8,128)(2,1)S(1)} %get-tuple-element.15) | data formatting | bytes 2097152
  73.2 0.7 copy.15
Async XLA Ops:
  1.4 0.9 %copy-start.3 = (bf16[1,256,256]{2,1,0:T(8,128)(2,1)S(1)}, bf16[1,256,256]{2,1,0:T(8,128)(2,1)}, u32[]{:S(2)}) copy-start(bf16[1,256,256]{2,1,0:T(8,128)(2,1)} %first_ref.1) | copy-start | bytes 393220
  2.3 1.2 %copy-start = (bf16[1,256,2048]{2,1,0:T(8,128)(2,1)S(1)}, bf16[1,256,2048]{2,1,0:T(8,128)(2,1)}, u32[]{:S(2)}) copy-start(bf16[1,256,2048]{2,1,0:T(8,128)(2,1)} %tokens_ref.1) | copy-start | bytes 3145732
  3.5 1.2 %copy-start.1 = (bf16[1,256,2048]{2,1,0:T(8,128)(2,1)S(1)}, bf16[1,256,2048]{2,1,0:T(8,128)(2,1)}, u32[]{:S(2)}) copy-start(bf16[1,256,2048]{2,1,0:T(8,128)(2,1)} %cotangent_ref.1) | copy-start | bytes 3145732
  4.7 1.2 %copy-start.2 = (bf16[256,2048]{1,0:T(8,128)(2,1)S(1)}, bf16[256,2048]{1,0:T(8,128)(2,1)}, u32[]{:S(2)}) copy-start(bf16[256,2048]{1,0:T(8,128)(2,1)} %kernel_ref.1) | copy-start | bytes 3145732

commit v2 on v1

--- a/solution.py
+++ b/solution.py
@@ -13,6 +13,7 @@
 F32 = jnp.float32
 HALVES = 2
 CHUNKS = 4
+AHEAD = 2
 
 
 def dot(left, right):
@@ -187,7 +188,8 @@
         mixed[k, :, 1] = dot(first_v[...], cotangent_v[k]).astype(BF16).reshape(n, block, width)
         if k == 0:
             pl.semaphore_wait(barrier, n + groups - 2)
-        peers(lambda target, k=k: out_copy(k, me, target).start())
+        if k < AHEAD:
+            peers(lambda target, k=k: out_copy(k, me, target).start())
         arrived[k, me] = mixed[k, me]
     for trio in loads:
         trio[2].wait()
@@ -205,6 +207,11 @@
 
     def transform(k, carry):
         peers(lambda source: out_copy(k, source, me).wait_recv())
+
+        @pl.when(k + AHEAD < chunks)
+        def _():
+            peers(lambda target: out_copy(k + AHEAD, me, target).start())
+
         mixed_in = arrived[k, :, 0].reshape(rows, width)
         mixed_up = arrived[k, :, 1].reshape(rows, width)
         forward = dot(factor_v[...], mixed_in)
@@ -327,7 +334,7 @@
     seq_share = 1.0 / math.sqrt(groups)
     factor_share = 1.0 / math.sqrt(2.0 * channels * groups)
     second = jnp.transpose(second_factor, (2, 0, 1)).reshape(n, rows).astype(F32)
-    any_spec = pl.BlockSpec(memory_space=pl.ANY)
+    any_spec = pl.BlockSpec(memory_space=pltpu.HBM)
     vmem_spec = pl.BlockSpec(memory_space=pltpu.VMEM)
     dma = pltpu.SemaphoreType.DMA
     kernel_grad, first_grad, second_grad = pl.pallas_call(

time: 74.2 us -> 75 us (1.011)
  Pallas kernels: 65.5 us -> 66.3 us
    pallas_call x1, Pallas kernels: 65.5 us -> 66.3 us  [fused(): pl.pallas_call(functools.partial(mixer_kernel, n, groups, chunks, seq_sha...]
where the time goes in v2:
time: 75 us; the launch traced here: 74.7 us
  Pallas kernels  66.3 us (88%)
  local copies, waits for them, and re-layouts  7.04 us (9%)
    pallas_call x1, Pallas kernels, fused(): pl.pallas_call(functools.partial(mixer_kernel, n, groups, chunks, seq_sha...  66.3 us
    unnamed x11, local copies, waits for them, and re-layouts  6.73 us

profile of v2, /device:TPU:0, one launch (start us, length us, event | category | flops | bytes accessed | tf_op | source)
XLA Modules:
  0.0 74.7 jit_solution(13031739530121270876)
XLA Ops:
  0.6 0.7 convert_bitcast_fusion
  1.4 0.0 copy-start.3
  1.4 0.1 copy.10
  1.5 0.1 reshape.17.second_ref
  1.6 0.7 copy-done.3
  2.3 0.0 copy-start
  2.3 1.2 %copy-done = bf16[1,256,2048]{2,1,0:T(8,128)(2,1)S(1)} copy-done((bf16[1,256,2048]{2,1,0:T(8,128)(2,1)S(1)}, bf16[1,256,2048]{2,1,0:T(8,128)(2,1)}, u32[]{:S(2)}) %copy-start) | copy-done | bytes 1048600
  3.5 0.0 copy-start.1
  3.5 1.2 %copy-done.1 = bf16[1,256,2048]{2,1,0:T(8,128)(2,1)S(1)} copy-done((bf16[1,256,2048]{2,1,0:T(8,128)(2,1)S(1)}, bf16[1,256,2048]{2,1,0:T(8,128)(2,1)}, u32[]{:S(2)}) %copy-start.1) | copy-done | bytes 1048600
  4.7 0.0 copy-start.2
  4.7 1.2 %copy-done.2 = bf16[256,2048]{1,0:T(8,128)(2,1)S(1)} copy-done((bf16[256,2048]{1,0:T(8,128)(2,1)S(1)}, bf16[256,2048]{1,0:T(8,128)(2,1)}, u32[]{:S(2)}) %copy-start.2) | copy-done | bytes 1048600
  5.9 66.3 %shard_map.76 = (bf16[256,2048]{1,0:T(8,128)(2,1)S(1)}, f32[8,2,16,256]{3,2,1,0:T(8,128)S(1)}, f32[8,256]{1,0:T(8,128)S(1)}) custom-call(bf16[1,256,2048]{2,1,0:T(8,128)(2,1)S(1)} %copy-done, bf16[1,256,2048]{2,1,0:T(8,128)(2,1)S(1)} %copy-done.1, bf16[256,2048]{1,0:T(8,128)(2,1)S(1)} %copy-done.2, bf16[1,256,256]{2,1,0:T(8,128)(2,1)S(1)} %copy-done.3, ...), custom_call_target="tpu_custom_call" | custom-call | flops 2147483648 | bytes 4194304 | tf_op jit(solution)/shard_map/pallas_call | solution.py:340
  72.2 0.1 reshape.16
  72.3 0.7 copy.11
  73.0 1.0 %copy.14 = bf16[256,2048]{1,0:T(8,128)(2,1)} copy(bf16[256,2048]{1,0:T(8,128)(2,1)S(1)} %get-tuple-element.15) | data formatting | bytes 2097152
  74.0 0.7 copy.15
Async XLA Ops:
  1.4 0.9 %copy-start.3 = (bf16[1,256,256]{2,1,0:T(8,128)(2,1)S(1)}, bf16[1,256,256]{2,1,0:T(8,128)(2,1)}, u32[]{:S(2)}) copy-start(bf16[1,256,256]{2,1,0:T(8,128)(2,1)} %first_ref.1) | copy-start | bytes 393220
  2.3 1.2 %copy-start = (bf16[1,256,2048]{2,1,0:T(8,128)(2,1)S(1)}, bf16[1,256,2048]{2,1,0:T(8,128)(2,1)}, u32[]{:S(2)}) copy-start(bf16[1,256,2048]{2,1,0:T(8,128)(2,1)} %tokens_ref.1) | copy-start | bytes 3145732
  3.5 1.2 %copy-start.1 = (bf16[1,256,2048]{2,1,0:T(8,128)(2,1)S(1)}, bf16[1,256,2048]{2,1,0:T(8,128)(2,1)}, u32[]{:S(2)}) copy-start(bf16[1,256,2048]{2,1,0:T(8,128)(2,1)} %cotangent_ref.1) | copy-start | bytes 3145732
  4.7 1.2 %copy-start.2 = (bf16[256,2048]{1,0:T(8,128)(2,1)S(1)}, bf16[256,2048]{1,0:T(8,128)(2,1)}, u32[]{:S(2)}) copy-start(bf16[256,2048]{1,0:T(8,128)(2,1)} %kernel_ref.1) | copy-start | bytes 3145732

commit v3 on v1

--- a/solution.py
+++ b/solution.py
@@ -11,7 +11,7 @@
 MESH = pl.DeviceIdType.MESH
 BF16 = jnp.bfloat16
 F32 = jnp.float32
-HALVES = 2
+PARTS = 4
 CHUNKS = 4
 
 
@@ -21,6 +21,14 @@
 
 def dot_rows(left, right):
     return lax.dot_general(left, right, (((1,), (1,)), ((), ())), preferred_element_type=F32)
+
+
+def flipped(index, mask):
+    result = 0
+    for bit in (1, 2, 4):
+        own, flip = lax.rem(index // bit, 2), lax.rem(mask // bit, 2)
+        result = result + bit * (own + flip - 2 * own * flip)
+    return result
 
 
 def mixer_kernel(
@@ -63,6 +71,8 @@
     out_recv,
     back_send,
     back_recv,
+    late_send,
+    late_recv,
     outer_send,
     outer_recv,
     pair_send,
@@ -81,7 +91,7 @@
     rows = first_v.shape[0]
     width = tokens_v.shape[2]
     block = rows // n
-    part = block // HALVES
+    part = block // PARTS
 
     first_load = pltpu.make_async_copy(first_ref.at[0], first_v, first_load_sem)
     first_load.start()
@@ -109,7 +119,11 @@
     row_block = lax.broadcasted_iota(jnp.int32, shape, 1) * n
     column = lax.broadcasted_iota(jnp.int32, shape, 2)
     same_block = jnp.logical_and(column >= row_block, column < row_block + n)
-    spread_factor = jnp.broadcast_to(second_ref[...][:, None, :], shape)
+    pick_block = lax.broadcasted_iota(jnp.int32, (block, rows), 0) * n
+    pick_column = lax.broadcasted_iota(jnp.int32, (block, rows), 1)
+    picks = [(pick_column == pick_block + p).astype(F32).astype(BF16) for p in range(n)]
+    second = sum(dot(second_ref[p], picks[p]) for p in range(n))
+    spread_factor = jnp.broadcast_to(second[:, None, :], shape)
     transposed = jnp.where(same_block, spread_factor, 0.0).reshape(rows, rows)
     factor_t_v[...] = transposed.astype(BF16)
     factor_v[...] = transposed.T.astype(BF16)
@@ -125,12 +139,22 @@
             device_id_type=MESH,
         )
 
-    def back_copy(h, k, source, target):
+    def back_copy(k, source, target):
         return pltpu.make_async_remote_copy(
-            src_ref=spread.at[h, k, target],
-            dst_ref=returned.at[h, k, source],
-            send_sem=back_send.at[h, k, target],
-            recv_sem=back_recv.at[h, k, source],
+            src_ref=spread.at[0, target, k],
+            dst_ref=returned.at[0, source, k],
+            send_sem=back_send.at[k, target],
+            recv_sem=back_recv.at[k, source],
+            device_id={"seq": target},
+            device_id_type=MESH,
+        )
+
+    def late_copy(h, source, target):
+        return pltpu.make_async_remote_copy(
+            src_ref=spread.at[h, target],
+            dst_ref=returned.at[h, source],
+            send_sem=late_send.at[h, target],
+            recv_sem=late_recv.at[h, source],
             device_id={"seq": target},
             device_id_type=MESH,
         )
@@ -169,11 +193,11 @@
         )
 
     def peers(action):
-        def step(d, carry):
-            action(lax.rem(me + d, n))
+        def step(i, carry):
+            action(flipped(me, 1 + lax.rem(2 * i + 1, n - 1)))
             return carry
 
-        lax.fori_loop(1, n, step, 0)
+        lax.fori_loop(0, n - 1, step, 0)
 
     def line_peers(action):
         for d in range(1, groups):
@@ -213,12 +237,11 @@
         gains = kernel_v[k].astype(F32)
         weighted = (gains * forward).astype(BF16)
         pulled = (gains * backward).astype(BF16)
-        back = dot(factor_t_v[...], pulled).astype(BF16).reshape(n, HALVES, part, width)
-        ahead = dot(factor_t_v[...], weighted).astype(BF16).reshape(n, HALVES, part, width)
-        for h in range(HALVES):
-            spread[h, k, :, 0] = back[:, h]
-            spread[h, k, :, 1] = ahead[:, h]
-        peers(lambda target: back_copy(0, k, me, target).start())
+        back = dot(factor_t_v[...], pulled).reshape(n, PARTS, part, width)
+        ahead = dot(factor_t_v[...], weighted).reshape(n, PARTS, part, width)
+        for h in range(PARTS):
+            spread[h, :, k] = jnp.concatenate([back[:, h], ahead[:, h]], axis=1).astype(BF16)
+        peers(lambda target: back_copy(k, me, target).start())
 
         @pl.when(outer)
         def _():
@@ -229,8 +252,6 @@
         def _():
             own_terms[k] = terms
 
-        for h in range(HALVES):
-            returned[h, k, me] = spread[h, k, me]
         second_acc[...] += dot_rows(mixed_in, pulled) + dot_rows(mixed_up, weighted)
 
         @pl.when(jnp.logical_and(inner, k >= 1))
@@ -244,9 +265,10 @@
         return carry
 
     lax.fori_loop(0, chunks, transform, 0)
-    for h in range(1, HALVES):
-        for k in range(chunks):
-            peers(lambda target, h=h, k=k: back_copy(h, k, me, target).start())
+    for h in range(1, PARTS):
+        peers(lambda target, h=h: late_copy(h, me, target).start())
+    for h in range(PARTS):
+        returned[h, me] = spread[h, me]
 
     second_terms[z] = jnp.sum(
         jnp.where(same_block, second_acc[...].reshape(shape), 0.0), axis=1
@@ -259,18 +281,22 @@
         if chunks >= 2:
             make_final(chunks - 2)
 
-    for h in range(HALVES):
+    for h in range(PARTS):
         first_acc[...] = jnp.zeros_like(first_acc)
+        if h > 0:
+            peers(lambda source, h=h: late_copy(h, source, me).wait_recv())
 
         def gather(k, carry, h=h):
-            peers(lambda source: back_copy(h, k, source, me).wait_recv())
-            back = returned[h, k, :, 0].reshape(n * part, width)
-            ahead = returned[h, k, :, 1].reshape(n * part, width)
-            first_acc[...] += dot_rows(back, tokens_v[k]) + dot_rows(ahead, cotangent_v[k])
+            if h == 0:
+                peers(lambda source: back_copy(k, source, me).wait_recv())
+            both = returned[h, :, k].reshape(n * 2 * part, width)
+            by_tokens = dot_rows(both, tokens_v[k]).reshape(n, 2, part, rows)
+            by_cotangent = dot_rows(both, cotangent_v[k]).reshape(n, 2, part, rows)
+            first_acc[...] += by_tokens[:, 0] + by_cotangent[:, 1]
             return carry
 
         lax.fori_loop(0, chunks, gather, 0)
-        first_terms[h, z] = first_acc[...].astype(BF16)
+        first_terms[h, z] = first_acc[...].reshape(n * part, rows).astype(BF16)
         line_peers(lambda target, h=h: first_copy(h, z, target).start())
         if h == 0:
 
@@ -278,6 +304,15 @@
             def _():
                 make_final(chunks - 1)
 
+            line_peers(lambda source: second_copy(source, z).wait_recv())
+            rest = jnp.sum(second_terms[...], axis=0) * factor_share
+            pieces = []
+            for _ in range(3):
+                pieces.append(rest.astype(BF16))
+                rest = rest - pieces[-1].astype(F32)
+            for p in range(n):
+                second_out[p] = sum(dot_rows(piece, picks[p]) for piece in reversed(pieces))
+
     stores = []
     for k in range(chunks):
 
@@ -290,9 +325,7 @@
         )
         stores[-1].start()
 
-    line_peers(lambda source: second_copy(source, z).wait_recv())
-    second_out[...] = jnp.sum(second_terms[...], axis=0) * factor_share
-    for h in range(HALVES):
+    for h in range(PARTS):
         line_peers(lambda source, h=h: first_copy(h, source, z).wait_recv())
         total = jnp.sum(first_terms[h].astype(F32), axis=0) * factor_share
         first_out[:, h] = total.reshape(n, part, rows)
@@ -301,8 +334,7 @@
         store.wait()
     for k in range(chunks):
         peers(lambda target, k=k: out_copy(k, me, target).wait_send())
-        for h in range(HALVES):
-            peers(lambda target, h=h, k=k: back_copy(h, k, me, target).wait_send())
+        peers(lambda target, k=k: back_copy(k, me, target).wait_send())
 
         @pl.when(outer)
         def _():
@@ -314,7 +346,9 @@
             final_copy(k).wait_send()
 
     line_peers(lambda target: second_copy(z, target).wait_send())
-    for h in range(HALVES):
+    for h in range(1, PARTS):
+        peers(lambda target, h=h: late_copy(h, me, target).wait_send())
+    for h in range(PARTS):
         line_peers(lambda target, h=h: first_copy(h, z, target).wait_send())
 
 
@@ -323,10 +357,10 @@
     chunks = CHUNKS
     width = channels // chunks
     block = rows // n
-    part = block // HALVES
+    part = block // PARTS
     seq_share = 1.0 / math.sqrt(groups)
     factor_share = 1.0 / math.sqrt(2.0 * channels * groups)
-    second = jnp.transpose(second_factor, (2, 0, 1)).reshape(n, rows).astype(F32)
+    second = jnp.transpose(second_factor, (1, 2, 0))
     any_spec = pl.BlockSpec(memory_space=pl.ANY)
     vmem_spec = pl.BlockSpec(memory_space=pltpu.VMEM)
     dma = pltpu.SemaphoreType.DMA
@@ -334,8 +368,8 @@
         functools.partial(mixer_kernel, n, groups, chunks, seq_share, factor_share),
         out_shape=(
             jax.ShapeDtypeStruct((rows, channels), BF16),
-            jax.ShapeDtypeStruct((n, HALVES, part, rows), F32),
-            jax.ShapeDtypeStruct((n, rows), F32),
+            jax.ShapeDtypeStruct((n, PARTS, part, rows), F32),
+            jax.ShapeDtypeStruct((n, n, block), F32),
         ),
         in_specs=[any_spec] * 4 + [vmem_spec],
         out_specs=(any_spec, vmem_spec, vmem_spec),
@@ -348,8 +382,8 @@
             pltpu.VMEM((rows, rows), BF16),
             pltpu.VMEM((chunks, n, 2, block, width), BF16),
             pltpu.VMEM((chunks, n, 2, block, width), BF16),
-            pltpu.VMEM((HALVES, chunks, n, 2, part, width), BF16),
-            pltpu.VMEM((HALVES, chunks, n, 2, part, width), BF16),
+            pltpu.VMEM((PARTS, n, chunks, 2 * part, width), BF16),
+            pltpu.VMEM((PARTS, n, chunks, 2 * part, width), BF16),
             pltpu.VMEM((chunks, rows, width), F32),
             pltpu.VMEM((chunks, rows, width), BF16),
             pltpu.VMEM((chunks, rows, width), BF16),
@@ -357,15 +391,17 @@
             pltpu.VMEM((chunks, rows, width), BF16),
             pltpu.VMEM((rows, rows), F32),
             pltpu.VMEM((groups, n, rows), F32),
-            pltpu.VMEM((n * part, rows), F32),
-            pltpu.VMEM((HALVES, groups, n * part, rows), BF16),
+            pltpu.VMEM((n, part, rows), F32),
+            pltpu.VMEM((PARTS, groups, n * part, rows), BF16),
             dma((chunks, 3)),
             dma,
             dma((chunks,)),
             dma((chunks, n)),
             dma((chunks, n)),
-            dma((HALVES, chunks, n)),
-            dma((HALVES, chunks, n)),
+            dma((chunks, n)),
+            dma((chunks, n)),
+            dma((PARTS, n)),
+            dma((PARTS, n)),
             dma((chunks,)),
             dma((chunks,)),
             dma((chunks,)),
@@ -374,17 +410,17 @@
             dma((chunks,)),
             dma((groups,)),
             dma((groups,)),
-            dma((HALVES, groups)),
-            dma((HALVES, groups)),
+            dma((PARTS, groups)),
+            dma((PARTS, groups)),
         ],
         compiler_params=pltpu.CompilerParams(
-            collective_id=0, has_side_effects=True, vmem_limit_bytes=48 * 1024 * 1024
+            collective_id=0, has_side_effects=True, vmem_limit_bytes=60 * 1024 * 1024
         ),
         cost_estimate=pl.CostEstimate(
             flops=16 * rows * rows * channels, bytes_accessed=8 * rows * channels, transcendentals=0
         ),
     )(tokens, cotangent, kernel, first_factor, second)
-    second_grad = second_grad.reshape(n, block, n).transpose(1, 2, 0)
+    second_grad = jnp.transpose(second_grad, (2, 0, 1))
     return kernel_grad, first_grad.reshape(1, rows, rows), second_grad
 
 
@@ -446,7 +482,8 @@
         groups == 4
         and first_factor.shape[0] == 1
         and second_factor.shape[1] == n
-        and second_factor.shape[0] % (16 * HALVES) == 0
+        and second_factor.shape[0] == 8 * PARTS
+        and n == 8
         and channels % (128 * CHUNKS) == 0
         and rows == n * second_factor.shape[0]
     )

time: 74.2 us -> 74.8 us (level)
  Pallas kernels: 65.5 us -> 70.2 us
  local copies, waits for them, and re-layouts: 7.04 us -> 3.72 us
    pallas_call x1, Pallas kernels: 65.5 us -> 70.2 us  [fused(): pl.pallas_call(functools.partial(mixer_kernel, n, groups, chunks, seq_sha...]
    unnamed x11 -> x7, local copies, waits for them, and re-layouts: 6.73 us -> 3.72 us
where the time goes in v3:
time: 74.8 us; the launch traced here: 74.5 us
  Pallas kernels  70.2 us (94%)
  local copies, waits for them, and re-layouts  3.72 us (5%)
    pallas_call x1, Pallas kernels, fused(): pl.pallas_call(functools.partial(mixer_kernel, n, groups, chunks, seq_sha...  70.2 us
    unnamed x7, local copies, waits for them, and re-layouts  3.72 us

profile of v3, /device:TPU:0, one launch (start us, length us, event | category | flops | bytes accessed | tf_op | source)
XLA Modules:
  0.0 74.5 jit_solution(6335330442516556679)
XLA Ops:
  0.6 70.2 %shard_map.76 = (bf16[256,2048]{1,0:T(8,128)(2,1)}, f32[8,4,8,256]{3,2,1,0:T(8,128)}, f32[8,8,32]{2,1,0:T(8,128)}) custom-call(bf16[1,256,2048]{2,1,0:T(8,128)(2,1)} %tokens_ref.1, bf16[1,256,2048]{2,1,0:T(8,128)(2,1)} %cotangent_ref.1, bf16[256,2048]{1,0:T(8,128)(2,1)} %kernel_ref.1, bf16[1,256,256]{2,1,0:T(8,128)(2,1)} %first_ref.1, bf16[8,8,32]{2,1,0:T(8,128)(2,1)} %bitcast.5), custom_call_target="tpu_custom_call" | custom-call | flops 2147483648 | bytes 4194304 | tf_op jit(solution)/shard_map/pallas_call | solution.py:367
  70.8 0.0 copy-start
  70.8 2.3 %copy.11 = bf16[256,2048]{1,0:T(8,128)(2,1)} copy(bf16[256,2048]{1,0:T(8,128)(2,1)} %get-tuple-element.12) | data formatting | bytes 2097152
  73.2 0.0 copy-done
  73.2 0.0 copy-start.1
  73.2 0.7 copy.12
  73.9 0.1 copy-done.1
  73.9 0.6 copy.13
Async XLA Ops:
  70.8 2.4 %copy-start = (f32[8,4,8,256]{3,2,1,0:T(8,128)S(1)}, f32[8,4,8,256]{3,2,1,0:T(8,128)}, u32[]{:S(2)}) copy-start(f32[8,4,8,256]{3,2,1,0:T(8,128)} %get-tuple-element.7) | copy-start | bytes 786436
  73.2 0.8 %copy-start.1 = (f32[8,8,32]{2,1,0:T(8,128)S(1)}, f32[8,8,32]{2,1,0:T(8,128)}, u32[]{:S(2)}) copy-start(f32[8,8,32]{2,1,0:T(8,128)} %get-tuple-element.8) | copy-start | bytes 24580

commit v4 on v1

--- a/solution.py
+++ b/solution.py
@@ -23,11 +23,18 @@
     return lax.dot_general(left, right, (((1,), (1,)), ((), ())), preferred_element_type=F32)
 
 
+def flipped(index, mask):
+    result = 0
+    for bit in (1, 2, 4):
+        own, flip = lax.rem(index // bit, 2), lax.rem(mask // bit, 2)
+        result = result + bit * (own + flip - 2 * own * flip)
+    return result
+
+
 def mixer_kernel(
     n,
     groups,
     chunks,
-    seq_share,
     factor_share,
     tokens_ref,
     cotangent_ref,
@@ -56,6 +63,8 @@
     second_terms,
     first_acc,
     first_terms,
+    first_in,
+    first_done,
     load_sem,
     first_load_sem,
     store_sem,
@@ -71,8 +80,10 @@
     final_recv,
     second_send,
     second_recv,
-    first_send,
-    first_recv,
+    scatter_send,
+    scatter_recv,
+    gather_send,
+    gather_recv,
 ):
     me = lax.axis_index("seq")
     z = lax.axis_index("dp")
@@ -109,7 +120,11 @@
     row_block = lax.broadcasted_iota(jnp.int32, shape, 1) * n
     column = lax.broadcasted_iota(jnp.int32, shape, 2)
     same_block = jnp.logical_and(column >= row_block, column < row_block + n)
-    spread_factor = jnp.broadcast_to(second_ref[...][:, None, :], shape)
+    pick_block = lax.broadcasted_iota(jnp.int32, (block, rows), 0) * n
+    pick_column = lax.broadcasted_iota(jnp.int32, (block, rows), 1)
+    picks = [(pick_column == pick_block + p).astype(F32).astype(BF16) for p in range(n)]
+    second = sum(dot(second_ref[p], picks[p]) for p in range(n))
+    spread_factor = jnp.broadcast_to(second[:, None, :], shape)
     transposed = jnp.where(same_block, spread_factor, 0.0).reshape(rows, rows)
     factor_t_v[...] = transposed.astype(BF16)
     factor_v[...] = transposed.T.astype(BF16)
@@ -163,17 +178,30 @@
             second_terms.at[source], second_terms.at[source], second_send.at[target], second_recv.at[source], target
         )
 
-    def first_copy(h, source, target):
+    def scatter_copy(h, source, target):
         return line_copy(
-            first_terms.at[h, source], first_terms.at[h, source], first_send.at[h, target], first_recv.at[h, source], target
+            first_terms.at[h, target],
+            first_in.at[h, source],
+            scatter_send.at[h, target],
+            scatter_recv.at[h, source],
+            target,
+        )
+
+    def gather_copy(h, source, target):
+        return line_copy(
+            first_done.at[h, source],
+            first_done.at[h, source],
+            gather_send.at[h, target],
+            gather_recv.at[h, source],
+            target,
         )
 
     def peers(action):
-        def step(d, carry):
-            action(lax.rem(me + d, n))
+        def step(i, carry):
+            action(flipped(me, 1 + lax.rem(2 * i + 1, n - 1)))
             return carry
 
-        lax.fori_loop(1, n, step, 0)
+        lax.fori_loop(0, n - 1, step, 0)
 
     def line_peers(action):
         for d in range(1, groups):
@@ -200,7 +228,7 @@
     def make_final(k):
         pair_copy(k).wait_recv()
         total = pair_terms[k].astype(F32) + other_terms[k].astype(F32)
-        final_terms[k] = (total * seq_share).astype(BF16)
+        final_terms[k] = total.astype(BF16)
         final_copy(k).start()
 
     def transform(k, carry):
@@ -213,22 +241,22 @@
         gains = kernel_v[k].astype(F32)
         weighted = (gains * forward).astype(BF16)
         pulled = (gains * backward).astype(BF16)
+
+        @pl.when(outer)
+        def _():
+            pair_terms[k] = terms.astype(BF16)
+            outer_copy(k).start()
+
+        @pl.when(inner)
+        def _():
+            own_terms[k] = terms
+
         back = dot(factor_t_v[...], pulled).astype(BF16).reshape(n, HALVES, part, width)
         ahead = dot(factor_t_v[...], weighted).astype(BF16).reshape(n, HALVES, part, width)
         for h in range(HALVES):
             spread[h, k, :, 0] = back[:, h]
             spread[h, k, :, 1] = ahead[:, h]
         peers(lambda target: back_copy(0, k, me, target).start())
-
-        @pl.when(outer)
-        def _():
-            pair_terms[k] = terms.astype(BF16)
-            outer_copy(k).start()
-
-        @pl.when(inner)
-        def _():
-            own_terms[k] = terms
-
         for h in range(HALVES):
             returned[h, k, me] = spread[h, k, me]
         second_acc[...] += dot_rows(mixed_in, pulled) + dot_rows(mixed_up, weighted)
@@ -244,10 +272,6 @@
         return carry
 
     lax.fori_loop(0, chunks, transform, 0)
-    for h in range(1, HALVES):
-        for k in range(chunks):
-            peers(lambda target, h=h, k=k: back_copy(h, k, me, target).start())
-
     second_terms[z] = jnp.sum(
         jnp.where(same_block, second_acc[...].reshape(shape), 0.0), axis=1
     )
@@ -259,24 +283,51 @@
         if chunks >= 2:
             make_final(chunks - 2)
 
-    for h in range(HALVES):
-        first_acc[...] = jnp.zeros_like(first_acc)
-
-        def gather(k, carry, h=h):
+    first_acc[...] = jnp.zeros_like(first_acc)
+
+    def gather(h):
+        def step(k, carry):
             peers(lambda source: back_copy(h, k, source, me).wait_recv())
+            if h + 1 < HALVES:
+                peers(lambda target: back_copy(h + 1, k, me, target).start())
             back = returned[h, k, :, 0].reshape(n * part, width)
             ahead = returned[h, k, :, 1].reshape(n * part, width)
-            first_acc[...] += dot_rows(back, tokens_v[k]) + dot_rows(ahead, cotangent_v[k])
+            first_acc[h] += dot_rows(back, tokens_v[k]) + dot_rows(ahead, cotangent_v[k])
             return carry
 
-        lax.fori_loop(0, chunks, gather, 0)
-        first_terms[h, z] = first_acc[...].astype(BF16)
-        line_peers(lambda target, h=h: first_copy(h, z, target).start())
-        if h == 0:
-
-            @pl.when(inner)
-            def _():
-                make_final(chunks - 1)
+        return step
+
+    def scatter(h):
+        first_terms[h] = first_acc[h].astype(BF16).reshape(groups, n * part // groups, rows)
+        line_peers(lambda target: scatter_copy(h, z, target).start())
+
+    def combine(h):
+        line_peers(lambda source: scatter_copy(h, source, z).wait_recv())
+        total = first_terms[h, z].astype(F32)
+        for d in range(1, groups):
+            total = total + first_in[h, lax.rem(z + d, groups)].astype(F32)
+        first_done[h, z] = total.astype(BF16)
+        line_peers(lambda target: gather_copy(h, z, target).start())
+
+    lax.fori_loop(0, chunks, gather(0), 0)
+
+    @pl.when(inner)
+    def _():
+        make_final(chunks - 1)
+
+    scatter(0)
+    line_peers(lambda source: second_copy(source, z).wait_recv())
+    rest = jnp.sum(second_terms[...], axis=0) * factor_share
+    pieces = []
+    for _ in range(3):
+        pieces.append(rest.astype(BF16))
+        rest = rest - pieces[-1].astype(F32)
+    for p in range(n):
+        second_out[p] = sum(dot_rows(piece, picks[p]) for piece in reversed(pieces))
+    lax.fori_loop(0, chunks // 2, gather(1), 0)
+    combine(0)
+    lax.fori_loop(chunks // 2, chunks, gather(1), 0)
+    scatter(1)
 
     stores = []
     for k in range(chunks):
@@ -290,12 +341,10 @@
         )
         stores[-1].start()
 
-    line_peers(lambda source: second_copy(source, z).wait_recv())
-    second_out[...] = jnp.sum(second_terms[...], axis=0) * factor_share
+    combine(1)
     for h in range(HALVES):
-        line_peers(lambda source, h=h: first_copy(h, source, z).wait_recv())
-        total = jnp.sum(first_terms[h].astype(F32), axis=0) * factor_share
-        first_out[:, h] = total.reshape(n, part, rows)
+        line_peers(lambda source, h=h: gather_copy(h, source, z).wait_recv())
+        first_out[:, h] = first_done[h].astype(F32).reshape(n, part, rows)
 
     for store in stores:
         store.wait()
@@ -315,7 +364,8 @@
 
     line_peers(lambda target: second_copy(z, target).wait_send())
     for h in range(HALVES):
-        line_peers(lambda target, h=h: first_copy(h, z, target).wait_send())
+        line_peers(lambda target, h=h: scatter_copy(h, z, target).wait_send())
+        line_peers(lambda target, h=h: gather_copy(h, z, target).wait_send())
 
 
 def fused(n, groups, tokens, cotangent, kernel, first_factor, second_factor):
@@ -326,16 +376,16 @@
     part = block // HALVES
     seq_share = 1.0 / math.sqrt(groups)
     factor_share = 1.0 / math.sqrt(2.0 * channels * groups)
-    second = jnp.transpose(second_factor, (2, 0, 1)).reshape(n, rows).astype(F32)
+    second = jnp.transpose(second_factor, (1, 2, 0))
     any_spec = pl.BlockSpec(memory_space=pl.ANY)
     vmem_spec = pl.BlockSpec(memory_space=pltpu.VMEM)
     dma = pltpu.SemaphoreType.DMA
     kernel_grad, first_grad, second_grad = pl.pallas_call(
-        functools.partial(mixer_kernel, n, groups, chunks, seq_share, factor_share),
+        functools.partial(mixer_kernel, n, groups, chunks, factor_share),
         out_shape=(
             jax.ShapeDtypeStruct((rows, channels), BF16),
             jax.ShapeDtypeStruct((n, HALVES, part, rows), F32),
-            jax.ShapeDtypeStruct((n, rows), F32),
+            jax.ShapeDtypeStruct((n, n, block), F32),
         ),
         in_specs=[any_spec] * 4 + [vmem_spec],
         out_specs=(any_spec, vmem_spec, vmem_spec),
@@ -357,8 +407,10 @@
             pltpu.VMEM((chunks, rows, width), BF16),
             pltpu.VMEM((rows, rows), F32),
             pltpu.VMEM((groups, n, rows), F32),
-            pltpu.VMEM((n * part, rows), F32),
-            pltpu.VMEM((HALVES, groups, n * part, rows), BF16),
+            pltpu.VMEM((HALVES, n * part, rows), F32),
+            pltpu.VMEM((HALVES, groups, n * part // groups, rows), BF16),
+            pltpu.VMEM((HALVES, groups, n * part // groups, rows), BF16),
+            pltpu.VMEM((HALVES, groups, n * part // groups, rows), BF16),
             dma((chunks, 3)),
             dma,
             dma((chunks,)),
@@ -376,16 +428,19 @@
             dma((groups,)),
             dma((HALVES, groups)),
             dma((HALVES, groups)),
+            dma((HALVES, groups)),
+            dma((HALVES, groups)),
         ],
         compiler_params=pltpu.CompilerParams(
-            collective_id=0, has_side_effects=True, vmem_limit_bytes=48 * 1024 * 1024
+            collective_id=0, has_side_effects=True, vmem_limit_bytes=60 * 1024 * 1024
         ),
         cost_estimate=pl.CostEstimate(
             flops=16 * rows * rows * channels, bytes_accessed=8 * rows * channels, transcendentals=0
         ),
     )(tokens, cotangent, kernel, first_factor, second)
-    second_grad = second_grad.reshape(n, block, n).transpose(1, 2, 0)
-    return kernel_grad, first_grad.reshape(1, rows, rows), second_grad
+    second_grad = jnp.transpose(second_grad, (2, 0, 1))
+    kernel_grad = (kernel_grad.astype(F32) * seq_share).astype(BF16)
+    return kernel_grad, first_grad.reshape(1, rows, rows) * factor_share, second_grad
 
 
 def separate(tokens, cotangent, kernel, first_factor, second_factor):
@@ -446,7 +501,8 @@
         groups == 4
         and first_factor.shape[0] == 1
         and second_factor.shape[1] == n
-        and second_factor.shape[0] % (16 * HALVES) == 0
+        and second_factor.shape[0] == 16 * HALVES
+        and n == 8
         and channels % (128 * CHUNKS) == 0
         and rows == n * second_factor.shape[0]
     )

time: 74.2 us -> 76.4 us (1.030)
  local copies, waits for them, and re-layouts: 7.04 us -> 0.62 us
  Pallas kernels: 65.5 us -> 71.7 us
  other arithmetic: 0.72 us -> 3.18 us
    pallas_call x1, Pallas kernels: 65.5 us -> 71.7 us  [fused(): pl.pallas_call(functools.partial(mixer_kernel, n, groups, chunks, factor_...]
    unnamed x11 -> x5, local copies, waits for them, and re-layouts: 6.73 us -> 0.62 us
    convert_element_type x1, other arithmetic: 0.72 us -> 2.45 us  [fused(): kernel_grad = (kernel_grad.astype(F32) * seq_share).astype(BF16)]
where the time goes in v4:
time: 76.4 us; the launch traced here: 76.1 us
  Pallas kernels  71.7 us (94%)
  other arithmetic  3.18 us (4%)
    pallas_call x1, Pallas kernels, fused(): pl.pallas_call(functools.partial(mixer_kernel, n, groups, chunks, factor_...  71.7 us
    convert_element_type x1, other arithmetic, fused(): kernel_grad = (kernel_grad.astype(F32) * seq_share).astype(BF16)  2.45 us

profile of v4, /device:TPU:0, one launch (start us, length us, event | category | flops | bytes accessed | tf_op | source)
XLA Modules:
  0.0 76.1 jit_solution(4905615031911950596)
XLA Ops:
  0.6 71.7 %shard_map.76 = (bf16[256,2048]{1,0:T(8,128)(2,1)}, f32[8,2,16,256]{3,2,1,0:T(8,128)}, f32[8,8,32]{2,1,0:T(8,128)}) custom-call(bf16[1,256,2048]{2,1,0:T(8,128)(2,1)} %tokens_ref.1, bf16[1,256,2048]{2,1,0:T(8,128)(2,1)} %cotangent_ref.1, bf16[256,2048]{1,0:T(8,128)(2,1)} %kernel_ref.1, bf16[1,256,256]{2,1,0:T(8,128)(2,1)} %first_ref.1, bf16[8,8,32]{2,1,0:T(8,128)(2,1)} %bitcast.5), custom_call_target="tpu_custom_call" | custom-call | flops 2147483648 | bytes 4194304 | tf_op jit(solution)/shard_map/pallas_call | solution.py:383
  72.3 0.0 copy-start
  72.3 0.0 copy-start.1
  72.3 2.5 %multiply_convert_fusion = bf16[256,2048]{1,0:T(8,128)(2,1)} fusion(bf16[256,2048]{1,0:T(8,128)(2,1)} %get-tuple-element.6), kind=kLoop, calls=%fused_computation | loop fusion | flops 1572864 | bytes 2097152 | tf_op jit(solution)/shard_map/convert_element_type | solution.py:442
  74.8 0.0 copy-done
  74.8 0.7 broadcast_multiply_fusion
  75.5 0.0 copy-done.1
  75.5 0.6 copy.9
Async XLA Ops:
  72.3 2.5 %copy-start = (f32[8,2,16,256]{3,2,1,0:T(8,128)S(1)}, f32[8,2,16,256]{3,2,1,0:T(8,128)}, u32[]{:S(2)}) copy-start(f32[8,2,16,256]{3,2,1,0:T(8,128)} %get-tuple-element.7) | copy-start | bytes 786436
  72.3 3.2 %copy-start.1 = (f32[8,8,32]{2,1,0:T(8,128)S(1)}, f32[8,8,32]{2,1,0:T(8,128)}, u32[]{:S(2)}) copy-start(f32[8,8,32]{2,1,0:T(8,128)} %get-tuple-element.8) | copy-start | bytes 24580

commit v5 on v4

--- a/solution.py
+++ b/solution.py
@@ -23,18 +23,20 @@
     return lax.dot_general(left, right, (((1,), (1,)), ((), ())), preferred_element_type=F32)
 
 
-def flipped(index, mask):
-    result = 0
-    for bit in (1, 2, 4):
-        own, flip = lax.rem(index // bit, 2), lax.rem(mask // bit, 2)
-        result = result + bit * (own + flip - 2 * own * flip)
-    return result
+def partner(index, mask):
+    core, x, y = lax.rem(index, 2), lax.rem(index // 2, 2), index // 4
+    flip_core, low, high = lax.rem(mask, 2), lax.rem(mask // 2, 2), mask // 4
+    flip_x = low * (1 - core) + high * core
+    flip_y = high * (1 - core) + low * core
+    flip = lambda own, by: own + by - 2 * own * by
+    return (flip(y, flip_y) * 2 + flip(x, flip_x)) * 2 + flip(core, flip_core)
 
 
 def mixer_kernel(
     n,
     groups,
     chunks,
+    seq_share,
     factor_share,
     tokens_ref,
     cotangent_ref,
@@ -198,7 +200,7 @@
 
     def peers(action):
         def step(i, carry):
-            action(flipped(me, 1 + lax.rem(2 * i + 1, n - 1)))
+            action(partner(me, 1 + lax.rem(2 * i + 1, n - 1)))
             return carry
 
         lax.fori_loop(0, n - 1, step, 0)
@@ -228,7 +230,7 @@
     def make_final(k):
         pair_copy(k).wait_recv()
         total = pair_terms[k].astype(F32) + other_terms[k].astype(F32)
-        final_terms[k] = total.astype(BF16)
+        final_terms[k] = (total * seq_share).astype(BF16)
         final_copy(k).start()
 
     def transform(k, carry):
@@ -272,6 +274,9 @@
         return carry
 
     lax.fori_loop(0, chunks, transform, 0)
+    for h in range(1, HALVES):
+        for k in range(chunks):
+            peers(lambda target, h=h, k=k: back_copy(h, k, me, target).start())
     second_terms[z] = jnp.sum(
         jnp.where(same_block, second_acc[...].reshape(shape), 0.0), axis=1
     )
@@ -288,8 +293,6 @@
     def gather(h):
         def step(k, carry):
             peers(lambda source: back_copy(h, k, source, me).wait_recv())
-            if h + 1 < HALVES:
-                peers(lambda target: back_copy(h + 1, k, me, target).start())
             back = returned[h, k, :, 0].reshape(n * part, width)
             ahead = returned[h, k, :, 1].reshape(n * part, width)
             first_acc[h] += dot_rows(back, tokens_v[k]) + dot_rows(ahead, cotangent_v[k])
@@ -344,7 +347,8 @@
     combine(1)
     for h in range(HALVES):
         line_peers(lambda source, h=h: gather_copy(h, source, z).wait_recv())
-        first_out[:, h] = first_done[h].astype(F32).reshape(n, part, rows)
+        total = first_done[h].astype(F32) * factor_share
+        first_out[:, h] = total.reshape(n, part, rows)
 
     for store in stores:
         store.wait()
@@ -366,6 +370,33 @@
     for h in range(HALVES):
         line_peers(lambda target, h=h: scatter_copy(h, z, target).wait_send())
         line_peers(lambda target, h=h: gather_copy(h, z, target).wait_send())
+
+
+def copies_kernel(pieces, *refs):
+    sources, results, sem = refs[: len(refs) // 2], refs[len(refs) // 2 : -1], refs[-1]
+    copies = []
+    for source, result in zip(sources, results, strict=True):
+        parts = pieces if source.ndim == 2 else 1
+        step = source.shape[0] // parts
+        for part in range(parts):
+            span = pl.ds(part * step, step)
+            copies.append(pltpu.make_async_copy(source.at[span], result.at[span], sem.at[len(copies)]))
+            copies[-1].start()
+    for copy in copies:
+        copy.wait()
+
+
+def handed_on(*arrays):
+    pieces = 4
+    any_spec = pl.BlockSpec(memory_space=pl.ANY)
+    return pl.pallas_call(
+        functools.partial(copies_kernel, pieces),
+        out_shape=tuple(jax.ShapeDtypeStruct(array.shape, array.dtype) for array in arrays),
+        in_specs=[any_spec] * len(arrays),
+        out_specs=(any_spec,) * len(arrays),
+        scratch_shapes=[pltpu.SemaphoreType.DMA((pieces + len(arrays),))],
+        compiler_params=pltpu.CompilerParams(vmem_limit_bytes=60 * 1024 * 1024),
+    )(*arrays)
 
 
 def fused(n, groups, tokens, cotangent, kernel, first_factor, second_factor):
@@ -381,7 +412,7 @@
     vmem_spec = pl.BlockSpec(memory_space=pltpu.VMEM)
     dma = pltpu.SemaphoreType.DMA
     kernel_grad, first_grad, second_grad = pl.pallas_call(
-        functools.partial(mixer_kernel, n, groups, chunks, factor_share),
+        functools.partial(mixer_kernel, n, groups, chunks, seq_share, factor_share),
         out_shape=(
             jax.ShapeDtypeStruct((rows, channels), BF16),
             jax.ShapeDtypeStruct((n, HALVES, part, rows), F32),
@@ -438,9 +469,9 @@
             flops=16 * rows * rows * channels, bytes_accessed=8 * rows * channels, transcendentals=0
         ),
     )(tokens, cotangent, kernel, first_factor, second)
+    kernel_grad, first_grad, second_grad = handed_on(kernel_grad, first_grad, second_grad)
     second_grad = jnp.transpose(second_grad, (2, 0, 1))
-    kernel_grad = (kernel_grad.astype(F32) * seq_share).astype(BF16)
-    return kernel_grad, first_grad.reshape(1, rows, rows) * factor_share, second_grad
+    return kernel_grad, first_grad.reshape(1, rows, rows), second_grad
 
 
 def separate(tokens, cotangent, kernel, first_factor, second_factor):

time: 76.4 us -> 116 us (1.52)
  Pallas kernels: 71.7 us -> 115 us
  other arithmetic: 3.18 us -> 0 us
    pallas_call x1 -> x2, Pallas kernels: 71.7 us -> 115 us  [the longest x1 72.7 us: fused(): pl.pallas_call(functools.partial(mixer_kernel, n, groups, chunks, seq_sha...]
    convert_element_type x1 -> x0, other arithmetic: 2.45 us -> none  [fused(): kernel_grad = (kernel_grad.astype(F32) * seq_share).astype(BF16)]
where the time goes in v5:
time: 116 us; the launch traced here: 115 us
  Pallas kernels  115 us (99%)
    pallas_call x1, Pallas kernels, fused(): pl.pallas_call(functools.partial(mixer_kernel, n, groups, chunks, seq_sha...  72.7 us
    pallas_call x1, Pallas kernels, handed_on(): pl.pallas_call(functools.partial(copies_kernel, pieces), out_shape=tuple(...  41.9 us

profile of v5, /device:TPU:0, one launch (start us, length us, event | category | flops | bytes accessed | tf_op | source)
XLA Modules:
  0.0 115.2 jit_solution(15387633995832238358)
XLA Ops:
  0.6 72.7 %shard_map.76 = (bf16[256,2048]{1,0:T(8,128)(2,1)}, f32[8,2,16,256]{3,2,1,0:T(8,128)}, f32[8,8,32]{2,1,0:T(8,128)}) custom-call(bf16[1,256,2048]{2,1,0:T(8,128)(2,1)} %tokens_ref.1, bf16[1,256,2048]{2,1,0:T(8,128)(2,1)} %cotangent_ref.1, bf16[256,2048]{1,0:T(8,128)(2,1)} %kernel_ref.1, bf16[1,256,256]{2,1,0:T(8,128)(2,1)} %first_ref.1, bf16[8,8,32]{2,1,0:T(8,128)(2,1)} %bitcast.5), custom_call_target="tpu_custom_call" | custom-call | flops 2147483648 | bytes 4194304 | tf_op jit(solution)/shard_map/pallas_call | solution.py:414
  73.4 41.9 %shard_map.77 = (bf16[256,2048]{1,0:T(8,128)(2,1)}, f32[8,2,16,256]{3,2,1,0:T(8,128)}, f32[8,8,32]{2,1,0:T(8,128)}) custom-call(bf16[256,2048]{1,0:T(8,128)(2,1)} %get-tuple-element.9.refs_0_, f32[8,2,16,256]{3,2,1,0:T(8,128)} %get-tuple-element.10.refs_1_, f32[8,8,32]{2,1,0:T(8,128)} %get-tuple-element.11.refs_2_), custom_call_target="tpu_custom_call" | custom-call | tf_op jit(solution)/shard_map/pallas_call | solution.py:392

commit v6 on v3

--- a/solution.py
+++ b/solution.py
@@ -13,6 +13,7 @@
 F32 = jnp.float32
 PARTS = 4
 CHUNKS = 4
+AHEAD = 2
 
 
 def dot(left, right):
@@ -23,12 +24,13 @@
     return lax.dot_general(left, right, (((1,), (1,)), ((), ())), preferred_element_type=F32)
 
 
-def flipped(index, mask):
-    result = 0
-    for bit in (1, 2, 4):
-        own, flip = lax.rem(index // bit, 2), lax.rem(mask // bit, 2)
-        result = result + bit * (own + flip - 2 * own * flip)
-    return result
+def partner(index, mask):
+    core, x, y = lax.rem(index, 2), lax.rem(index // 2, 2), index // 4
+    flip_core, low, high = lax.rem(mask, 2), lax.rem(mask // 2, 2), mask // 4
+    flip_x = low * (1 - core) + high * core
+    flip_y = high * (1 - core) + low * core
+    flip = lambda own, by: own + by - 2 * own * by
+    return (flip(y, flip_y) * 2 + flip(x, flip_x)) * 2 + flip(core, flip_core)
 
 
 def mixer_kernel(
@@ -194,7 +196,7 @@
 
     def peers(action):
         def step(i, carry):
-            action(flipped(me, 1 + lax.rem(2 * i + 1, n - 1)))
+            action(partner(me, 1 + lax.rem(2 * i + 1, n - 1)))
             return carry
 
         lax.fori_loop(0, n - 1, step, 0)
@@ -211,7 +213,8 @@
         mixed[k, :, 1] = dot(first_v[...], cotangent_v[k]).astype(BF16).reshape(n, block, width)
         if k == 0:
             pl.semaphore_wait(barrier, n + groups - 2)
-        peers(lambda target, k=k: out_copy(k, me, target).start())
+        if k < AHEAD:
+            peers(lambda target, k=k: out_copy(k, me, target).start())
         arrived[k, me] = mixed[k, me]
     for trio in loads:
         trio[2].wait()
@@ -229,6 +232,11 @@
 
     def transform(k, carry):
         peers(lambda source: out_copy(k, source, me).wait_recv())
+
+        @pl.when(k + AHEAD < chunks)
+        def _():
+            peers(lambda target: out_copy(k + AHEAD, me, target).start())
+
         mixed_in = arrived[k, :, 0].reshape(rows, width)
         mixed_up = arrived[k, :, 1].reshape(rows, width)
         forward = dot(factor_v[...], mixed_in)
@@ -254,13 +262,13 @@
 
         second_acc[...] += dot_rows(mixed_in, pulled) + dot_rows(mixed_up, weighted)
 
-        @pl.when(jnp.logical_and(inner, k >= 1))
-        def _():
-            make_pair(k - 1)
-
         @pl.when(jnp.logical_and(inner, k >= 2))
         def _():
-            make_final(k - 2)
+            make_pair(k - 2)
+
+        @pl.when(jnp.logical_and(inner, k >= 3))
+        def _():
+            make_final(k - 3)
 
         return carry
 
@@ -277,9 +285,8 @@
 
     @pl.when(inner)
     def _():
-        make_pair(chunks - 1)
-        if chunks >= 2:
-            make_final(chunks - 2)
+        make_pair(chunks - 2)
+        make_final(chunks - 3)
 
     for h in range(PARTS):
         first_acc[...] = jnp.zeros_like(first_acc)
@@ -295,7 +302,15 @@
             first_acc[...] += by_tokens[:, 0] + by_cotangent[:, 1]
             return carry
 
-        lax.fori_loop(0, chunks, gather, 0)
+        lax.fori_loop(0, chunks // 2, gather, 0)
+        if h == 0:
+
+            @pl.when(inner)
+            def _():
+                make_pair(chunks - 1)
+                make_final(chunks - 2)
+
+        lax.fori_loop(chunks // 2, chunks, gather, 0)
         first_terms[h, z] = first_acc[...].reshape(n * part, rows).astype(BF16)
         line_peers(lambda target, h=h: first_copy(h, z, target).start())
         if h == 0:

time: 74.8 us -> 80.3 us (1.074)
  Pallas kernels: 70.2 us -> 75.6 us
    pallas_call x1, Pallas kernels: 70.2 us -> 75.6 us  [fused(): pl.pallas_call(functools.partial(mixer_kernel, n, groups, chunks, seq_sha...]
where the time goes in v6:
time: 80.3 us; the launch traced here: 79.9 us
  Pallas kernels  75.6 us (94%)
  local copies, waits for them, and re-layouts  3.72 us (5%)
    pallas_call x1, Pallas kernels, fused(): pl.pallas_call(functools.partial(mixer_kernel, n, groups, chunks, seq_sha...  75.6 us
    unnamed x7, local copies, waits for them, and re-layouts  3.72 us

profile of v6, /device:TPU:0, one launch (start us, length us, event | category | flops | bytes accessed | tf_op | source)
XLA Modules:
  0.0 79.9 jit_solution(13785917747879406058)
XLA Ops:
  0.6 75.6 %shard_map.76 = (bf16[256,2048]{1,0:T(8,128)(2,1)}, f32[8,4,8,256]{3,2,1,0:T(8,128)}, f32[8,8,32]{2,1,0:T(8,128)}) custom-call(bf16[1,256,2048]{2,1,0:T(8,128)(2,1)} %tokens_ref.1, bf16[1,256,2048]{2,1,0:T(8,128)(2,1)} %cotangent_ref.1, bf16[256,2048]{1,0:T(8,128)(2,1)} %kernel_ref.1, bf16[1,256,256]{2,1,0:T(8,128)(2,1)} %first_ref.1, bf16[8,8,32]{2,1,0:T(8,128)(2,1)} %bitcast.5), custom_call_target="tpu_custom_call" | custom-call | flops 2147483648 | bytes 4194304 | tf_op jit(solution)/shard_map/pallas_call | solution.py:382
  76.2 0.0 copy-start
  76.2 2.3 %copy.11 = bf16[256,2048]{1,0:T(8,128)(2,1)} copy(bf16[256,2048]{1,0:T(8,128)(2,1)} %get-tuple-element.12) | data formatting | bytes 2097152
  78.6 0.0 copy-done
  78.6 0.0 copy-start.1
  78.6 0.7 copy.12
  79.3 0.1 copy-done.1
  79.3 0.6 copy.13
Async XLA Ops:
  76.2 2.4 %copy-start = (f32[8,4,8,256]{3,2,1,0:T(8,128)S(1)}, f32[8,4,8,256]{3,2,1,0:T(8,128)}, u32[]{:S(2)}) copy-start(f32[8,4,8,256]{3,2,1,0:T(8,128)} %get-tuple-element.7) | copy-start | bytes 786436
  78.6 0.8 copy-start.1

commit v7 on v1

--- a/solution.py
+++ b/solution.py
@@ -12,7 +12,8 @@
 BF16 = jnp.bfloat16
 F32 = jnp.float32
 HALVES = 2
-CHUNKS = 4
+CHUNKS = 8
+LAG = 4
 
 
 def dot(left, right):
@@ -109,7 +110,11 @@
     row_block = lax.broadcasted_iota(jnp.int32, shape, 1) * n
     column = lax.broadcasted_iota(jnp.int32, shape, 2)
     same_block = jnp.logical_and(column >= row_block, column < row_block + n)
-    spread_factor = jnp.broadcast_to(second_ref[...][:, None, :], shape)
+    pick_block = lax.broadcasted_iota(jnp.int32, (block, rows), 0) * n
+    pick_column = lax.broadcasted_iota(jnp.int32, (block, rows), 1)
+    picks = [(pick_column == pick_block + p).astype(F32).astype(BF16) for p in range(n)]
+    second = sum(dot(second_ref[p], picks[p]) for p in range(n))
+    spread_factor = jnp.broadcast_to(second[:, None, :], shape)
     transposed = jnp.where(same_block, spread_factor, 0.0).reshape(rows, rows)
     factor_t_v[...] = transposed.astype(BF16)
     factor_v[...] = transposed.T.astype(BF16)
@@ -233,13 +238,9 @@
             returned[h, k, me] = spread[h, k, me]
         second_acc[...] += dot_rows(mixed_in, pulled) + dot_rows(mixed_up, weighted)
 
-        @pl.when(jnp.logical_and(inner, k >= 1))
-        def _():
-            make_pair(k - 1)
-
-        @pl.when(jnp.logical_and(inner, k >= 2))
-        def _():
-            make_final(k - 2)
+        @pl.when(jnp.logical_and(inner, k >= LAG))
+        def _():
+            make_pair(k - LAG)
 
         return carry
 
@@ -255,9 +256,12 @@
 
     @pl.when(inner)
     def _():
-        make_pair(chunks - 1)
-        if chunks >= 2:
-            make_final(chunks - 2)
+        def follow(k, carry):
+            make_pair(k + LAG)
+            make_final(k)
+            return carry
+
+        lax.fori_loop(0, chunks - LAG, follow, 0)
 
     for h in range(HALVES):
         first_acc[...] = jnp.zeros_like(first_acc)
@@ -272,11 +276,25 @@
         lax.fori_loop(0, chunks, gather, 0)
         first_terms[h, z] = first_acc[...].astype(BF16)
         line_peers(lambda target, h=h: first_copy(h, z, target).start())
+
+        @pl.when(inner)
+        def _():
+            def follow(k, carry):
+                make_final(k)
+                return carry
+
+            last = chunks - 1
+            lax.fori_loop(chunks - LAG if h == 0 else last, last if h == 0 else chunks, follow, 0)
+
         if h == 0:
-
-            @pl.when(inner)
-            def _():
-                make_final(chunks - 1)
+            line_peers(lambda source: second_copy(source, z).wait_recv())
+            rest = jnp.sum(second_terms[...], axis=0) * factor_share
+            pieces = []
+            for _ in range(3):
+                pieces.append(rest.astype(BF16))
+                rest = rest - pieces[-1].astype(F32)
+            for p in range(n):
+                second_out[p] = sum(dot_rows(piece, picks[p]) for piece in reversed(pieces))
 
     stores = []
     for k in range(chunks):
@@ -290,8 +308,6 @@
         )
         stores[-1].start()
 
-    line_peers(lambda source: second_copy(source, z).wait_recv())
-    second_out[...] = jnp.sum(second_terms[...], axis=0) * factor_share
     for h in range(HALVES):
         line_peers(lambda source, h=h: first_copy(h, source, z).wait_recv())
         total = jnp.sum(first_terms[h].astype(F32), axis=0) * factor_share
@@ -326,7 +342,7 @@
     part = block // HALVES
     seq_share = 1.0 / math.sqrt(groups)
     factor_share = 1.0 / math.sqrt(2.0 * channels * groups)
-    second = jnp.transpose(second_factor, (2, 0, 1)).reshape(n, rows).astype(F32)
+    second = jnp.transpose(second_factor, (1, 2, 0))
     any_spec = pl.BlockSpec(memory_space=pl.ANY)
     vmem_spec = pl.BlockSpec(memory_space=pltpu.VMEM)
     dma = pltpu.SemaphoreType.DMA
@@ -335,7 +351,7 @@
         out_shape=(
             jax.ShapeDtypeStruct((rows, channels), BF16),
             jax.ShapeDtypeStruct((n, HALVES, part, rows), F32),
-            jax.ShapeDtypeStruct((n, rows), F32),
+            jax.ShapeDtypeStruct((n, n, block), F32),
         ),
         in_specs=[any_spec] * 4 + [vmem_spec],
         out_specs=(any_spec, vmem_spec, vmem_spec),
@@ -378,13 +394,13 @@
             dma((HALVES, groups)),
         ],
         compiler_params=pltpu.CompilerParams(
-            collective_id=0, has_side_effects=True, vmem_limit_bytes=48 * 1024 * 1024
+            collective_id=0, has_side_effects=True, vmem_limit_bytes=60 * 1024 * 1024
         ),
         cost_estimate=pl.CostEstimate(
             flops=16 * rows * rows * channels, bytes_accessed=8 * rows * channels, transcendentals=0
         ),
     )(tokens, cotangent, kernel, first_factor, second)
-    second_grad = second_grad.reshape(n, block, n).transpose(1, 2, 0)
+    second_grad = jnp.transpose(second_grad, (2, 0, 1))
     return kernel_grad, first_grad.reshape(1, rows, rows), second_grad
 
 

time: 74.2 us -> 77.7 us (1.047)
  Pallas kernels: 65.5 us -> 73.1 us
  local copies, waits for them, and re-layouts: 7.04 us -> 3.72 us
    pallas_call x1, Pallas kernels: 65.5 us -> 73.1 us  [fused(): pl.pallas_call(functools.partial(mixer_kernel, n, groups, chunks, seq_sha...]
    unnamed x11 -> x7, local copies, waits for them, and re-layouts: 6.73 us -> 3.72 us
where the time goes in v7:
time: 77.7 us; the launch traced here: 77.5 us
  Pallas kernels  73.1 us (94%)
  local copies, waits for them, and re-layouts  3.72 us (5%)
    pallas_call x1, Pallas kernels, fused(): pl.pallas_call(functools.partial(mixer_kernel, n, groups, chunks, seq_sha...  73.1 us
    unnamed x7, local copies, waits for them, and re-layouts  3.72 us

profile of v7, /device:TPU:0, one launch (start us, length us, event | category | flops | bytes accessed | tf_op | source)
XLA Modules:
  0.0 77.5 jit_solution(2462731242244721463)
XLA Ops:
  0.6 73.1 %shard_map.76 = (bf16[256,2048]{1,0:T(8,128)(2,1)}, f32[8,2,16,256]{3,2,1,0:T(8,128)}, f32[8,8,32]{2,1,0:T(8,128)}) custom-call(bf16[1,256,2048]{2,1,0:T(8,128)(2,1)} %tokens_ref.1, bf16[1,256,2048]{2,1,0:T(8,128)(2,1)} %cotangent_ref.1, bf16[256,2048]{1,0:T(8,128)(2,1)} %kernel_ref.1, bf16[1,256,256]{2,1,0:T(8,128)(2,1)} %first_ref.1, bf16[8,8,32]{2,1,0:T(8,128)(2,1)} %bitcast.5), custom_call_target="tpu_custom_call" | custom-call | flops 2147483648 | bytes 4194304 | tf_op jit(solution)/shard_map/pallas_call | solution.py:349
  73.7 0.0 copy-start
  73.7 2.3 %copy.11 = bf16[256,2048]{1,0:T(8,128)(2,1)} copy(bf16[256,2048]{1,0:T(8,128)(2,1)} %get-tuple-element.12) | data formatting | bytes 2097152
  76.1 0.0 copy-done
  76.1 0.0 copy-start.1
  76.1 0.7 copy.12
  76.8 0.1 copy-done.1
  76.9 0.6 copy.13
Async XLA Ops:
  73.7 2.4 %copy-start = (f32[8,2,16,256]{3,2,1,0:T(8,128)S(1)}, f32[8,2,16,256]{3,2,1,0:T(8,128)}, u32[]{:S(2)}) copy-start(f32[8,2,16,256]{3,2,1,0:T(8,128)} %get-tuple-element.7) | copy-start | bytes 786436
  76.1 0.8 copy-start.1

commit v8 on v1

--- a/solution.py
+++ b/solution.py
@@ -109,7 +109,11 @@
     row_block = lax.broadcasted_iota(jnp.int32, shape, 1) * n
     column = lax.broadcasted_iota(jnp.int32, shape, 2)
     same_block = jnp.logical_and(column >= row_block, column < row_block + n)
-    spread_factor = jnp.broadcast_to(second_ref[...][:, None, :], shape)
+    pick_block = lax.broadcasted_iota(jnp.int32, (block, rows), 0) * n
+    pick_column = lax.broadcasted_iota(jnp.int32, (block, rows), 1)
+    picks = [(pick_column == pick_block + p).astype(F32).astype(BF16) for p in range(n)]
+    second = sum(dot(second_ref[p], picks[p]) for p in range(n))
+    spread_factor = jnp.broadcast_to(second[:, None, :], shape)
     transposed = jnp.where(same_block, spread_factor, 0.0).reshape(rows, rows)
     factor_t_v[...] = transposed.astype(BF16)
     factor_v[...] = transposed.T.astype(BF16)
@@ -278,6 +282,15 @@
             def _():
                 make_final(chunks - 1)
 
+    line_peers(lambda source: second_copy(source, z).wait_recv())
+    rest = jnp.sum(second_terms[...], axis=0) * factor_share
+    pieces = []
+    for _ in range(3):
+        pieces.append(rest.astype(BF16))
+        rest = rest - pieces[-1].astype(F32)
+    for p in range(n):
+        second_out[p] = sum(dot_rows(piece, picks[p]) for piece in reversed(pieces))
+
     stores = []
     for k in range(chunks):
 
@@ -290,8 +303,6 @@
         )
         stores[-1].start()
 
-    line_peers(lambda source: second_copy(source, z).wait_recv())
-    second_out[...] = jnp.sum(second_terms[...], axis=0) * factor_share
     for h in range(HALVES):
         line_peers(lambda source, h=h: first_copy(h, source, z).wait_recv())
         total = jnp.sum(first_terms[h].astype(F32), axis=0) * factor_share
@@ -326,7 +337,7 @@
     part = block // HALVES
     seq_share = 1.0 / math.sqrt(groups)
     factor_share = 1.0 / math.sqrt(2.0 * channels * groups)
-    second = jnp.transpose(second_factor, (2, 0, 1)).reshape(n, rows).astype(F32)
+    second = jnp.transpose(second_factor, (1, 2, 0))
     any_spec = pl.BlockSpec(memory_space=pl.ANY)
     vmem_spec = pl.BlockSpec(memory_space=pltpu.VMEM)
     dma = pltpu.SemaphoreType.DMA
@@ -335,7 +346,7 @@
         out_shape=(
             jax.ShapeDtypeStruct((rows, channels), BF16),
             jax.ShapeDtypeStruct((n, HALVES, part, rows), F32),
-            jax.ShapeDtypeStruct((n, rows), F32),
+            jax.ShapeDtypeStruct((n, n, block), F32),
         ),
         in_specs=[any_spec] * 4 + [vmem_spec],
         out_specs=(any_spec, vmem_spec, vmem_spec),
@@ -384,7 +395,7 @@
             flops=16 * rows * rows * channels, bytes_accessed=8 * rows * channels, transcendentals=0
         ),
     )(tokens, cotangent, kernel, first_factor, second)
-    second_grad = second_grad.reshape(n, block, n).transpose(1, 2, 0)
+    second_grad = jnp.transpose(second_grad, (2, 0, 1))
     return kernel_grad, first_grad.reshape(1, rows, rows), second_grad
 
 

time: 74.2 us -> 74 us (level)
    unnamed x11 -> x13, local copies, waits for them, and re-layouts: 6.73 us -> 7.58 us
where the time goes in v8:
time: 74 us; the launch traced here: 73.7 us
  Pallas kernels  65.5 us (89%)
  local copies, waits for them, and re-layouts  7.58 us (10%)
    pallas_call x1, Pallas kernels, fused(): pl.pallas_call(functools.partial(mixer_kernel, n, groups, chunks, seq_sha...  65.5 us
    unnamed x13, local copies, waits for them, and re-layouts  7.58 us

profile of v8, /device:TPU:0, one launch (start us, length us, event | category | flops | bytes accessed | tf_op | source)
XLA Modules:
  0.0 73.7 jit_solution(3624328320123629274)
XLA Ops:
  0.6 0.0 copy-start
  0.6 1.2 %copy-done = bf16[1,256,2048]{2,1,0:T(8,128)(2,1)S(1)} copy-done((bf16[1,256,2048]{2,1,0:T(8,128)(2,1)S(1)}, bf16[1,256,2048]{2,1,0:T(8,128)(2,1)}, u32[]{:S(2)}) %copy-start) | copy-done | bytes 1048600
  1.9 0.0 copy-start.1
  1.9 1.2 %copy-done.1 = bf16[1,256,2048]{2,1,0:T(8,128)(2,1)S(1)} copy-done((bf16[1,256,2048]{2,1,0:T(8,128)(2,1)S(1)}, bf16[1,256,2048]{2,1,0:T(8,128)(2,1)}, u32[]{:S(2)}) %copy-start.1) | copy-done | bytes 1048600
  3.1 0.0 copy-start.2
  3.1 1.2 %copy-done.2 = bf16[256,2048]{1,0:T(8,128)(2,1)S(1)} copy-done((bf16[256,2048]{1,0:T(8,128)(2,1)S(1)}, bf16[256,2048]{1,0:T(8,128)(2,1)}, u32[]{:S(2)}) %copy-start.2) | copy-done | bytes 1048600
  4.3 0.0 copy-start.3
  4.3 0.9 %copy-done.3 = bf16[1,256,256]{2,1,0:T(8,128)(2,1)S(1)} copy-done((bf16[1,256,256]{2,1,0:T(8,128)(2,1)S(1)}, bf16[1,256,256]{2,1,0:T(8,128)(2,1)}, u32[]{:S(2)}) %copy-start.3) | copy-done | bytes 131096
  5.2 0.0 copy-start.4
  5.2 0.7 copy-done.4
  5.9 65.5 %shard_map.76 = (bf16[256,2048]{1,0:T(8,128)(2,1)S(1)}, f32[8,2,16,256]{3,2,1,0:T(8,128)S(1)}, f32[8,8,32]{2,1,0:T(8,128)S(1)}) custom-call(bf16[1,256,2048]{2,1,0:T(8,128)(2,1)S(1)} %copy-done, bf16[1,256,2048]{2,1,0:T(8,128)(2,1)S(1)} %copy-done.1, bf16[256,2048]{1,0:T(8,128)(2,1)S(1)} %copy-done.2, bf16[1,256,256]{2,1,0:T(8,128)(2,1)S(1)} %copy-done.3, ...), custom_call_target="tpu_custom_call" | custom-call | flops 2147483648 | bytes 4194304 | tf_op jit(solution)/shard_map/pallas_call | solution.py:344
  71.4 1.0 %copy.11 = bf16[256,2048]{1,0:T(8,128)(2,1)} copy(bf16[256,2048]{1,0:T(8,128)(2,1)S(1)} %get-tuple-element.12) | data formatting | bytes 2097152
  72.4 0.7 copy.12
  73.1 0.6 copy.13
Async XLA Ops:
  0.6 1.2 %copy-start = (bf16[1,256,2048]{2,1,0:T(8,128)(2,1)S(1)}, bf16[1,256,2048]{2,1,0:T(8,128)(2,1)}, u32[]{:S(2)}) copy-start(bf16[1,256,2048]{2,1,0:T(8,128)(2,1)} %tokens_ref.1) | copy-start | bytes 3145732
  1.9 1.2 %copy-start.1 = (bf16[1,256,2048]{2,1,0:T(8,128)(2,1)S(1)}, bf16[1,256,2048]{2,1,0:T(8,128)(2,1)}, u32[]{:S(2)}) copy-start(bf16[1,256,2048]{2,1,0:T(8,128)(2,1)} %cotangent_ref.1) | copy-start | bytes 3145732
  3.1 1.2 %copy-start.2 = (bf16[256,2048]{1,0:T(8,128)(2,1)S(1)}, bf16[256,2048]{1,0:T(8,128)(2,1)}, u32[]{:S(2)}) copy-start(bf16[256,2048]{1,0:T(8,128)(2,1)} %kernel_ref.1) | copy-start | bytes 3145732
  4.3 0.9 %copy-start.3 = (bf16[1,256,256]{2,1,0:T(8,128)(2,1)S(1)}, bf16[1,256,256]{2,1,0:T(8,128)(2,1)}, u32[]{:S(2)}) copy-start(bf16[1,256,256]{2,1,0:T(8,128)(2,1)} %first_ref.1) | copy-start | bytes 393220
  5.2 0.7 copy-start.4

commit v9 on v8

--- a/solution.py
+++ b/solution.py
@@ -389,7 +389,7 @@
             dma((HALVES, groups)),
         ],
         compiler_params=pltpu.CompilerParams(
-            collective_id=0, has_side_effects=True, vmem_limit_bytes=48 * 1024 * 1024
+            collective_id=0, has_side_effects=True, vmem_limit_bytes=60 * 1024 * 1024
         ),
         cost_estimate=pl.CostEstimate(
             flops=16 * rows * rows * channels, bytes_accessed=8 * rows * channels, transcendentals=0

time: 74 us -> 70.5 us (0.953)
  local copies, waits for them, and re-layouts: 7.58 us -> 3.72 us
    unnamed x13 -> x7, local copies, waits for them, and re-layouts: 7.58 us -> 3.72 us
where the time goes in v9:
time: 70.5 us; the launch traced here: 69.8 us
  Pallas kernels  65.5 us (93%)
  local copies, waits for them, and re-layouts  3.72 us (5%)
    pallas_call x1, Pallas kernels, fused(): pl.pallas_call(functools.partial(mixer_kernel, n, groups, chunks, seq_sha...  65.5 us
    unnamed x7, local copies, waits for them, and re-layouts  3.72 us

profile of v9, /device:TPU:0, one launch (start us, length us, event | category | flops | bytes accessed | tf_op | source)
XLA Modules:
  0.0 69.8 jit_solution(10743191626355322771)
XLA Ops:
  0.6 65.5 %shard_map.76 = (bf16[256,2048]{1,0:T(8,128)(2,1)}, f32[8,2,16,256]{3,2,1,0:T(8,128)}, f32[8,8,32]{2,1,0:T(8,128)}) custom-call(bf16[1,256,2048]{2,1,0:T(8,128)(2,1)} %tokens_ref.1, bf16[1,256,2048]{2,1,0:T(8,128)(2,1)} %cotangent_ref.1, bf16[256,2048]{1,0:T(8,128)(2,1)} %kernel_ref.1, bf16[1,256,256]{2,1,0:T(8,128)(2,1)} %first_ref.1, bf16[8,8,32]{2,1,0:T(8,128)(2,1)} %bitcast.5), custom_call_target="tpu_custom_call" | custom-call | flops 2147483648 | bytes 4194304 | tf_op jit(solution)/shard_map/pallas_call | solution.py:344
  66.1 0.0 copy-start
  66.1 2.3 %copy.11 = bf16[256,2048]{1,0:T(8,128)(2,1)} copy(bf16[256,2048]{1,0:T(8,128)(2,1)} %get-tuple-element.12) | data formatting | bytes 2097152
  68.5 0.0 copy-done
  68.5 0.0 copy-start.1
  68.5 0.7 %copy.12 = f32[1,256,256]{2,1,0:T(8,128)} copy(f32[1,256,256]{2,1,0:T(8,128)S(1)} %bitcast.3) | data formatting | bytes 524288
  69.2 0.1 copy-done.1
  69.2 0.6 copy.13
Async XLA Ops:
  66.1 2.4 %copy-start = (f32[8,2,16,256]{3,2,1,0:T(8,128)S(1)}, f32[8,2,16,256]{3,2,1,0:T(8,128)}, u32[]{:S(2)}) copy-start(f32[8,2,16,256]{3,2,1,0:T(8,128)} %get-tuple-element.7) | copy-start | bytes 786436
  68.5 0.8 %copy-start.1 = (f32[8,8,32]{2,1,0:T(8,128)S(1)}, f32[8,8,32]{2,1,0:T(8,128)}, u32[]{:S(2)}) copy-start(f32[8,8,32]{2,1,0:T(8,128)} %get-tuple-element.8) | copy-start | bytes 24580
